TPU v7x, 32 devices: a whole 2x2x4 slice. The times are simulated.
32 devices in a mesh: chan: 2 (over x), grid: 8 (over z, core), vis: 2 (over y).
Axes of the slice: x: 2, y: 2, z: 4, core: 2. Of those that a mesh axis runs over, the one named last changes fastest.
Arguments:
- model_grid: bfloat16 [4, 1024, 8192], P('chan', 'grid'), parts along dimension 0, may hold values from -6 to 6
- kernels: float32 [32, 28], replicated, may hold values from -1.5 to 1.5
- cover: int32 [4, 32], P(('chan', 'vis')), parts along dimension 0, may hold values from 0 to 511, as said below
- cells: int32 [4, 32, 6144], P(('chan', 'vis'), None, 'grid'), parts along dimension 0, may hold values from 0 to 15609, as said below
- planes: int32 [4, 32, 6144], P(('chan', 'vis'), None, 'grid'), parts along dimension 0, may hold values from 0 to 31
- observed: float32 [4, 2, 32, 6144], P('chan', 'vis', None, 'grid'), parts along dimension 0, may hold values from -6 to 6
- weights: float32 [4, 32, 6144], P(('chan', 'vis'), None, 'grid'), parts along dimension 0, may hold values from 0.2 to 2
Outputs:
- residual_grid: float32 [4, 1024, 8192], P('chan', 'grid', 'vis'), parts along dimension 0
There are 2 independent parts, one for each index of `chan`. A program takes and returns all parts, laid end to end along the dimension named above; an argument that names none is the same for every part. Nothing has to cross between parts.
Inputs may be any that keep to these rules, and one draw needn't show every extreme that they name: `cover`: each row lists 32 different patch numbers below 512; patch p lies in grid rows (p // 64) * 128 onward, the tile of one grid device. In every row, 2 tiles hold exactly 8 listed patches, 4 tiles hold 4 and the others none; which tiles, and the order of the list, vary from row to row. cells = r * 128 + c with 0 <= r <= 121 and 0 <= c <= 121, so that every kernel lies inside its patch.
All inputs are finite; a program needn't handle non-finite values.
Results may differ from a plain program's by a relative error of at most 0.0043.
Values may be sent and summed in bfloat16 or wider, within the bound.
No kernel may reach another device: no remote copies, remote signals or barrier semaphores. Data moves between devices by JAX's collectives and lax.ppermute only.
A program may use at most 64 MiB of HBM per device.

v0:
```python
import jax
import jax.numpy as jnp
from jax import lax
from jax.sharding import PartitionSpec as P

PW = 128


def residual_patch(patch_cells, observed_pair, weight_row, cell_row, plane_row, kernels):
    rows_in = patch_cells.shape[1]
    cols_in = patch_cells.shape[2]
    support = kernels.shape[1] // 4
    planes_all = kernels.shape[0]
    count_rows = cell_row.shape[0]
    row_off = cell_row // cols_in
    col_off = cell_row % cols_in
    plane_hot = (plane_row[:, None] == jnp.arange(planes_all, dtype=jnp.int32)[None, :]).astype(
        jnp.float32
    )
    taps = jnp.dot(plane_hot, kernels, precision=lax.Precision.HIGHEST)
    u_dist = jnp.arange(rows_in, dtype=jnp.int32)[None, :] - row_off[:, None]
    v_dist = jnp.arange(cols_in, dtype=jnp.int32)[None, :] - col_off[:, None]
    u_real = jnp.zeros((count_rows, rows_in), jnp.float32)
    u_imag = jnp.zeros((count_rows, rows_in), jnp.float32)
    v_real = jnp.zeros((count_rows, cols_in), jnp.float32)
    v_imag = jnp.zeros((count_rows, cols_in), jnp.float32)
    for offset in range(support):
        u_hit = u_dist == offset
        v_hit = v_dist == offset
        u_real = u_real + jnp.where(u_hit, taps[:, offset : offset + 1], 0.0)
        u_imag = u_imag + jnp.where(u_hit, taps[:, support + offset : support + offset + 1], 0.0)
        v_real = v_real + jnp.where(
            v_hit, taps[:, 2 * support + offset : 2 * support + offset + 1], 0.0
        )
        v_imag = v_imag + jnp.where(
            v_hit, taps[:, 3 * support + offset : 3 * support + offset + 1], 0.0
        )
    u_rows = jnp.concatenate([u_real, u_imag], axis=1).astype(jnp.bfloat16)
    real_part = patch_cells[0]
    imag_part = patch_cells[1]
    upper = jnp.concatenate([real_part, imag_part], axis=1)
    lower = jnp.concatenate([-imag_part, real_part], axis=1)
    w_matrix = jnp.concatenate([upper, lower], axis=0)
    product = jnp.dot(u_rows, w_matrix, preferred_element_type=jnp.float32)
    m_real = product[:, :cols_in]
    m_imag = product[:, cols_in:]
    model_re = jnp.sum(m_real * v_real - m_imag * v_imag, axis=1)
    model_im = jnp.sum(m_real * v_imag + m_imag * v_real, axis=1)
    res_re = weight_row * (observed_pair[0] - model_re)
    res_im = weight_row * (observed_pair[1] - model_im)
    s_real = res_re[:, None] * v_real + res_im[:, None] * v_imag
    s_imag = res_im[:, None] * v_real - res_re[:, None] * v_imag
    s_rows = jnp.concatenate([s_real, s_imag], axis=1).astype(jnp.bfloat16)
    q_matrix = lax.dot_general(
        u_rows, s_rows, (((0,), (0,)), ((), ())), preferred_element_type=jnp.float32
    )
    q_real = q_matrix[:rows_in, :cols_in] + q_matrix[rows_in:, cols_in:]
    q_imag = q_matrix[:rows_in, cols_in:] - q_matrix[rows_in:, :cols_in]
    return jnp.stack([q_real, q_imag])


def shards(model_grid, kernels, cover, cells, planes, observed, weights):
    patch_rows = model_grid.shape[1]
    grid_cols = model_grid.shape[2]
    per_tile = grid_cols // PW
    grid_count = lax.axis_size("grid")
    this_tile = lax.axis_index("grid")
    listed = cover[0]
    cover_count = listed.shape[0]
    capacity = 2 * cover_count // grid_count
    owner_of = listed // per_tile
    column = listed % per_tile
    entry_ids = jnp.arange(cover_count, dtype=jnp.int32)
    shared = owner_of[:, None] == owner_of[None, :]
    earlier = entry_ids[None, :] < entry_ids[:, None]
    slot_rank = jnp.sum(jnp.where(shared & earlier, 1, 0), axis=1).astype(jnp.int32)
    slot_ids = jnp.arange(capacity, dtype=jnp.int32)
    own_select = (owner_of[None, :] == this_tile) & (slot_rank[None, :] == slot_ids[:, None])
    own_filled = jnp.any(own_select, axis=1)
    own_column = jnp.sum(jnp.where(own_select, column[None, :], 0), axis=1)
    own_column = jnp.where(own_filled, own_column, per_tile)
    tile_view = model_grid.reshape(2, patch_rows, per_tile, PW)
    float_data = jnp.concatenate(
        [jnp.transpose(observed[:, 0], (1, 0, 2)), weights[0][:, None, :]], axis=1
    )
    index_data = jnp.stack([cells[0], planes[0]], axis=1)

    def one_slot(item):
        patch_cells, floats_in, indices_in = item
        return residual_patch(
            patch_cells, floats_in[0:2], floats_in[2], indices_in[0], indices_in[1], kernels
        )

    owned_hot = (
        (owner_of == this_tile)[:, None]
        & (column[:, None] == jnp.arange(per_tile, dtype=jnp.int32)[None, :])
    ).astype(jnp.bfloat16)
    mine = jnp.einsum("ip,crpw->icrw", owned_hot, tile_view, preferred_element_type=jnp.bfloat16)
    fetched = lax.psum(mine, "grid").astype(jnp.float32).astype(jnp.bfloat16)
    partial_value = lax.map(one_slot, (fetched, float_data, index_data))
    totals = lax.psum(partial_value, "grid")
    own_slots = jnp.einsum(
        "ki,icrw->kcrw", own_select.astype(jnp.float32), totals, precision=lax.Precision.HIGHEST
    )
    vis_count = lax.axis_size("vis")
    slab_index = lax.axis_index("vis")
    per_slab = per_tile // vis_count
    slot_data = lax.all_gather(own_slots, "vis", axis=0, tiled=True)
    slot_columns = lax.all_gather(own_column, "vis", axis=0, tiled=True)
    local = slot_columns - slab_index * per_slab
    matches = (local[:, None] == jnp.arange(per_slab, dtype=jnp.int32)[None, :]).astype(jnp.float32)
    summed = jnp.einsum("jp,jcrw->crpw", matches, slot_data, precision=lax.Precision.HIGHEST)
    result = summed.reshape(2, patch_rows, per_slab * PW)
    return result


def solution(mesh):
    placed = (
        P("chan", "grid", None),
        P(),
        P(("chan", "vis"), None),
        P(("chan", "vis"), None, "grid"),
        P(("chan", "vis"), None, "grid"),
        P("chan", "vis", None, "grid"),
        P(("chan", "vis"), None, "grid"),
    )
    return jax.shard_map(
        shards, mesh=mesh, in_specs=placed, out_specs=P("chan", "grid", "vis"), check_vma=False
    )
```

profile of v0, /device:TPU:0, one launch (start us, length us, event | category | flops | bytes accessed | tf_op | source)
XLA Modules:
  0.0 403.2 jit_solution(2650865469178041412)
XLA Ops:
  7.9 3.4 copy.15
  11.3 0.8 fusion.35
  12.1 2.1 copy.11
  15.1 66.9 %all-reduce.4.cloned.1.call-done = bf16[32,2,128,128]{3,2,1,0:T(8,128)(2,1)} async-done(((bf16[32,2,128,128]{3,2,1,0:T(8,128)(2,1)}), bf16[32,2,128,128]{3,2,1,0:T(8,128)(2,1)}) %all-reduce.4.cloned.1.call-update) | async-done | bytes 2097168 | tf_op jit(solution)/shard_map/psum | solution.py:99
  81.9 168.0 %while.12 = (s32[]{:T(128)}, f32[32,2,128,128]{3,2,1,0:T(8,128)}, s32[32,2,768]{2,1,0:T(2,128)S(1)}, f32[32,28]{1,0:T(8,128)S(1)}, f32[32,3,768]{2,1,0:T(4,128)S...) while((s32[]{:T(128)}, f32[32,2,128,128]{3,2,1,0:T(8,128)}, ...), condition=%wide.region_5.6_spmd, body=%wide.region_2.5_spmd.sunk | while | flops 224386816 | bytes 5195933 | solution.py:100
  83.2 0.8 fusion.71
  83.9 0.8 dynamic-slice_bitcast_fusion.4
  88.4 0.8 fusion.71
  89.2 0.8 dynamic-slice_bitcast_fusion.4
  93.7 0.8 fusion.71
  94.5 0.8 dynamic-slice_bitcast_fusion.4
  98.9 0.8 fusion.71
  99.7 0.8 dynamic-slice_bitcast_fusion.4
  104.2 0.8 fusion.71
  105.0 0.8 dynamic-slice_bitcast_fusion.4
  109.4 0.8 fusion.71
  114.7 0.8 fusion.71
  119.9 0.8 fusion.71
  125.2 0.8 fusion.71
  130.4 0.8 fusion.71
  135.7 0.8 fusion.71
  140.9 0.8 fusion.71
  146.2 0.8 fusion.71
  151.4 0.8 fusion.71
  156.7 0.8 fusion.71
  161.9 0.8 fusion.71
  167.2 0.8 fusion.71
  172.4 0.8 fusion.71
  177.7 0.8 fusion.71
  182.9 0.8 fusion.71
  188.2 0.8 fusion.71
  193.4 0.8 fusion.71
  198.7 0.8 fusion.71
  203.9 0.8 fusion.71
  209.2 0.8 fusion.71
  214.4 0.8 fusion.71
  219.7 0.8 fusion.71
  224.9 0.8 fusion.71
  230.2 0.8 fusion.71
  235.4 0.8 fusion.71
  240.7 0.8 fusion.71
  245.9 0.8 fusion.71
  250.8 95.5 %all-reduce.6.cloned.1.call-done = f32[32,2,128,128]{3,2,1,0:T(8,128)} async-done(((f32[32,2,128,128]{3,2,1,0:T(8,128)}), f32[32,2,128,128]{3,2,1,0:T(8,128)}) %all-reduce.6.cloned.1.call-update) | async-done | bytes 4194320 | tf_op jit(solution)/shard_map/psum | solution.py:101
  346.3 6.7 %fusion.37 = f32[8,2,128,128]{3,0,2,1:T(8,128)} fusion(f32[32,2,128,128]{3,2,1,0:T(8,128)} %all-reduce.6.cloned.1.call-done, s32[32]{0:T(128)S(1)} %select_reduce_fusion, pred[32]{0:T(512)(128)(4,1)S(1)} %get-tuple-element.135), kind=kOutput, calls=%fused_computation.95 | convolution fusion | flops 100663808 | bytes 5243040 | tf_op jit(solution)/shard_map/ki,icrw->kcrw/dot_general | solution.py:102
  354.8 4.3 %all-reduce = s32[16]{0:T(128)S(1)} all-reduce(s32[16]{0:T(128)S(1)} %select_dynamic-update-slice_fusion), channel_id=1, replica_groups=mesh['chan'=2,'grid'=8,'vis'=2] {'vis'}, use_global_device_ids=true, to_apply=%add | all-reduce | flops 16 | bytes 128
  359.1 27.3 %all-gather.2.cloned.1.call-done = f32[16,2,128,128]{3,0,2,1:T(8,128)} async-done(((f32[8,2,128,128]{3,0,2,1:T(8,128)}), f32[16,2,128,128]{3,0,2,1:T(8,128)}) %all-gather.2.cloned.1.call-update) | async-done | bytes 2097168 | tf_op jit(solution)/shard_map/all_gather | solution.py:108
  386.4 5.4 %convolution_bitcast_fusion = f32[2,128,32,128]{3,2,1,0:T(8,128)} fusion(f32[16,2,128,128]{3,0,2,1:T(8,128)} %all-gather.2.cloned.1.call-done, s32[16]{0:T(128)S(1)} %broadcast_subtract_fusion), kind=kOutput, calls=%fused_computation.97 | convolution fusion | flops 201327104 | bytes 6291520 | tf_op jit(solution)/shard_map/jp,jcrw->crpw/dot_general | solution.py:112
  391.8 4.9 %reshape.173 = f32[2,128,4096]{2,1,0:T(8,128)} reshape(f32[2,128,32,128]{3,2,1,0:T(8,128)} %convolution_bitcast_fusion) | data formatting | bytes 8388608 | tf_op jit(solution)/shard_map/reshape | solution.py:113
  (513 shorter events, 141.0 us)
Async XLA Ops:
  6.5 75.4 %all-reduce.4.cloned.1.call-start = ((), (), s32[]{:S(2)}) async-start(), calls=%async_computation | async-start | bytes 4194304 | tf_op jit(solution)/shard_map/psum | solution.py:99
  12.0 2.3 copy-start.1
  12.0 2.4 copy-start.2
  12.1 2.5 copy-start.3
  12.1 2.6 copy-start.4
  12.1 69.9 %copy-start = (f32[32,28]{1,0:T(8,128)S(1)}, f32[32,28]{1,0:T(8,128)}, u32[]{:S(2)}) copy-start(f32[32,28]{1,0:T(8,128)} %param.10) | copy-start | bytes 10756
  14.2 332.1 %all-reduce.6.cloned.1.call-start = ((), (), s32[]{:S(2)}) async-start(), calls=%async_computation.1 | async-start | bytes 8388608 | tf_op jit(solution)/shard_map/psum | solution.py:101
  250.0 0.7 copy-start.5
  250.0 103.1 %copy-start.6 = (u32[32]{0:T(128)S(1)}, u32[32]{0:T(128)}, u32[]{:S(2)}) copy-start(u32[32]{0:T(128)} %constant.145) | copy-start | bytes 388
  250.0 136.4 %all-gather.2.cloned.1.call-start = ((), (), s32[]{:S(2)}) async-start(), calls=%async_computation.2 | async-start | bytes 3145728 | tf_op jit(solution)/shard_map/all_gather | solution.py:108
Sparse Core Ops, SparseCore 0:
  14.3 67.5 all-reduce.3
  250.1 96.1 all-reduce.5
  353.2 33.1 all-gather.1
where the time goes:
time: 408 us; the launch traced here: 403 us
  waiting for transfers between devices  190 us (47%)
  other arithmetic  99.9 us (24%)
  matrix products  46.8 us (11%)
  local copies, waits for them, and re-layouts  46 us (11%)
  between operations  14 us (3%)
  blocking collectives  4.25 us (1%)
    psum x1, waiting for transfers between devices, shards(): totals = lax.psum(partial_value, 'grid')  95.5 us
    psum x1, waiting for transfers between devices, shards(): fetched = lax.psum(mine, 'grid').astype(jnp.float32).astype(jnp.bfloat16)  66.9 us
    another operation x64, other arithmetic  32.6 us
    all_gather x1, waiting for transfers between devices, shards(): slot_data = lax.all_gather(own_slots, 'vis', axis=0, tiled=True)  27.3 us
    neg x32, other arithmetic, residual_patch(): lower = jnp.concatenate([-imag_part, real_part], axis=1)  24.8 us
    squeeze x32, local copies, waits for them, and re-layouts, residual_patch(): real_part = patch_cells[0]  24.3 us
    dynamic_update_slice x32, other arithmetic, shards(): partial_value = lax.map(one_slot, (fetched, float_data, index_data))  21.5 us
    reduce_sum x32, other arithmetic, residual_patch(): model_re = jnp.sum(m_real * v_real - m_imag * v_imag, axis=1)  17.8 us
  transfers between devices with their start and end apart: 3, of which 3 were waited for; matrix products, arithmetic and copies ran while one was open for 0% of the time, Pallas kernels for 0%

commit v1 on v0

v1 whole, which is shorter than its diff:
```python
import functools

import jax
import jax.numpy as jnp
from jax import lax
from jax.experimental import pallas as pl
from jax.experimental.pallas import tpu as pltpu
from jax.sharding import PartitionSpec as P

PW = 128
LANES = 128
FIELDS = 6
BF16 = jnp.bfloat16
F32 = jnp.float32
I32 = jnp.int32
VMEM_LIMIT = 48 * 1024 * 1024
EMPTY = 255


def round_up(value, unit):
    return -(-value // unit) * unit


def iota(shape, dim):
    return lax.broadcasted_iota(I32, shape, dim)


def pack_kernel(
    place_ref, cover_ref, cells_ref, planes_ref, observed_ref, weights_ref,
    *refs, count, tiles, per_tile, per_slab, capacity, rows,
):
    info_ref = refs[0]
    outs = refs[1:]
    me = place_ref[0]
    slab = place_ref[1]
    cover_row = cover_ref[...]
    across = jnp.broadcast_to(cover_row, (count, count))
    left = iota((count, count), 0)
    right = iota((count, count), 1)
    cover_col = jnp.sum(jnp.where(left == right, across, 0), axis=1, keepdims=True)

    def order_key(patch, entry):
        owner = patch // per_tile
        foreign = jnp.where((patch - owner * per_tile) // per_slab == slab, 1, 0)
        return owner, foreign * count + entry

    owner_i, key_i = order_key(cover_col, iota((count, 1), 0))
    owner_j, key_j = order_key(cover_row, iota((1, count), 1))
    same = owner_i == owner_j
    rank_row = jnp.sum(jnp.where(same & (key_i < key_j), 1, 0), axis=0, keepdims=True)
    rank_col = jnp.sum(jnp.where(same & (key_j < key_i), 1, 0), axis=1, keepdims=True)

    slot = iota((count, LANES), 1)
    own = (owner_i == me) & (rank_col == slot)
    column = cover_col - owner_i * per_tile
    listed = jnp.sum(jnp.where(own, column + 1, 0), axis=0, keepdims=True)
    total = jnp.sum(jnp.where(owner_i == me, 1, 0), axis=0, keepdims=True)
    lane = iota((1, LANES), 1)
    info = jnp.where(lane < capacity, listed - 1, jnp.where(lane == capacity, total, 0))
    info_ref[...] = jnp.broadcast_to(info, info_ref.shape)

    route = (owner_j ^ me) * capacity + rank_row
    spread = (iota((count, FIELDS * count), 1) % count == iota((count, FIELDS * count), 0)).astype(F32)
    wide = jnp.dot(
        jnp.broadcast_to(route.astype(F32), (8, count)).astype(BF16), spread.astype(BF16),
        preferred_element_type=F32,
    )[0:1].astype(I32)
    field_j = iota((1, FIELDS * count), 1) // count

    cells = cells_ref[0]
    row_off = cells // PW
    data = jnp.concatenate(
        [
            row_off.astype(F32).astype(BF16),
            (cells - row_off * PW).astype(F32).astype(BF16),
            planes_ref[0].astype(F32).astype(BF16),
            observed_ref[0, 0].astype(BF16),
            observed_ref[1, 0].astype(BF16),
            weights_ref[0].astype(BF16),
        ],
        axis=0,
    )
    line = iota((rows, FIELDS * count), 0)
    for m in range(tiles):
        field_i = line // capacity
        pick = (field_i == field_j) & (wide == m * capacity + line - field_i * capacity)
        block = jnp.dot(pick.astype(F32).astype(BF16), data, preferred_element_type=F32)
        outs[m][...] = block.astype(BF16)


def pack(place, cover, cells, planes, observed, weights, tiles, per_tile, per_slab):
    count, slots = cells.shape[1:]
    capacity = 2 * count // tiles
    rows = round_up(FIELDS * capacity, 16)
    whole = lambda shape: pl.BlockSpec(shape, lambda i, p: (0,) * len(shape))
    return pl.pallas_call(
        functools.partial(
            pack_kernel, count=count, tiles=tiles, per_tile=per_tile, per_slab=per_slab,
            capacity=capacity, rows=rows,
        ),
        grid_spec=pltpu.PrefetchScalarGridSpec(
            num_scalar_prefetch=1,
            grid=(1,),
            in_specs=[whole(a.shape) for a in (cover, cells, planes, observed, weights)],
            out_specs=[whole((8, LANES))] + [whole((rows, slots))] * tiles,
        ),
        out_shape=[jax.ShapeDtypeStruct((8, LANES), I32)]
        + [jax.ShapeDtypeStruct((rows, slots), BF16)] * tiles,
        compiler_params=pltpu.CompilerParams(vmem_limit_bytes=VMEM_LIMIT),
        name="pack_by_tile",
    )(place, cover, cells, planes, observed, weights)


def fill_tables(kern_ref, wide_ref, table_ref, support):
    wide_ref[...] = jnp.zeros_like(wide_ref)
    wide_ref[0 : kern_ref.shape[0], 0 : kern_ref.shape[1]] = kern_ref[...]
    flipped = wide_ref[...].T
    zero = jnp.zeros((8 - support, LANES), F32)
    for group in range(4):
        taps = flipped[support * group : support * (group + 1)]
        table_ref[group] = jnp.concatenate([taps, zero], axis=0)


def pick(array, index, axis):
    return jnp.take_along_axis(array, index, axis=axis)


def tap_places(offset):
    wide = jnp.broadcast_to(offset, (16, LANES))
    s = iota((16, LANES), 0)
    return jnp.minimum((s - wide) & 15, 7), (wide + 15 - s) >> 4


def wrapped(taps, places):
    return jnp.concatenate([pick(taps, places[0:8], 0), pick(taps, places[8:16], 0)], axis=0)


def expand(ref, base, cols, rows, group):
    group = group.astype(F32).astype(BF16)
    for q in range(PW // 16):
        ref[base + 16 * q : base + 16 * q + 16, cols] = jnp.where(group == BF16(q), rows, BF16(0))


def degrid_start(f_ref, item, table_ref, wt_ref, u_ref, m_ref, v_ref, g_ref):
    for t in range(u_ref.shape[1] // LANES):
        cols = pl.ds(t * LANES, LANES)
        row_off = f_ref[item, 0:1, cols].astype(I32)
        col_off = f_ref[item, 1:2, cols].astype(I32)
        plane = jnp.broadcast_to(f_ref[item, 2:3, cols].astype(I32), (8, LANES))
        u_place, u_group = tap_places(row_off)
        v_place, v_group = tap_places(col_off)
        u_re = wrapped(pick(table_ref[0], plane, 1), u_place).astype(BF16)
        u_im = wrapped(pick(table_ref[1], plane, 1), u_place).astype(BF16)
        v_ref[0, :, cols] = wrapped(pick(table_ref[2], plane, 1), v_place)
        v_ref[1, :, cols] = wrapped(pick(table_ref[3], plane, 1), v_place)
        g_ref[:, cols] = v_group
        expand(u_ref, 0, cols, u_re, u_group)
        expand(u_ref, PW, cols, u_im, u_group)
    m_ref[...] = jnp.dot(wt_ref[...], u_ref[...], preferred_element_type=F32)


def degrid_end(f_ref, item, u_ref, m_ref, s_ref, v_ref, g_ref, q_ref):
    for t in range(u_ref.shape[1] // LANES):
        cols = pl.ds(t * LANES, LANES)
        group = g_ref[:, cols]
        m_re = jnp.zeros((16, LANES), F32)
        m_im = jnp.zeros((16, LANES), F32)
        for q in range(PW // 16):
            hit = group == q
            m_re = jnp.where(hit, m_ref[16 * q : 16 * q + 16, cols], m_re)
            m_im = jnp.where(hit, m_ref[PW + 16 * q : PW + 16 * q + 16, cols], m_im)
        v_re = v_ref[0, :, cols]
        v_im = v_ref[1, :, cols]
        model_re = jnp.sum(m_re * v_re - m_im * v_im, axis=0, keepdims=True)
        model_im = jnp.sum(m_re * v_im + m_im * v_re, axis=0, keepdims=True)
        weight = f_ref[item, 5:6, cols]
        res_re = weight * (f_ref[item, 3:4, cols] - model_re)
        res_im = weight * (f_ref[item, 4:5, cols] - model_im)
        s_re = (res_re * v_re + res_im * v_im).astype(BF16)
        s_im = (res_im * v_re - res_re * v_im).astype(BF16)
        expand(s_ref, 0, cols, s_re, group)
        expand(s_ref, PW, cols, s_im, group)
    q_ref[...] += lax.dot_general(
        u_ref[...], s_ref[...], (((1,), (1,)), ((), ())), preferred_element_type=F32
    )


def residual_kernel(info_ref, *refs, blocks, capacity, support):
    block_refs = refs[:blocks]
    model_ref, kern_ref, patch_ref, send_ref = refs[blocks : blocks + 4]
    f_ref, table_ref, wide_ref, wt_ref, u_ref, m_ref, s_ref, v_ref, g_ref, q_ref = refs[blocks + 4 :]
    k = pl.program_id(0)

    @pl.when(k == 0)
    def _():
        fill_tables(kern_ref, wide_ref, table_ref, support)
        shape = (8 * capacity, block_refs[0].shape[0])
        line = iota(shape, 0)
        order = (iota(shape, 1) == (line & 7) * capacity + (line >> 3)).astype(F32).astype(BF16)
        for b in range(blocks):
            fields = jnp.dot(order, block_refs[b][...], preferred_element_type=F32)
            for slot in range(capacity):
                f_ref[b * capacity + slot] = fields[8 * slot : 8 * slot + 8]

    @pl.when(k < info_ref[0, capacity])
    def _():
        real = model_ref[0].T
        imag = model_ref[1].T
        wt_ref[0:PW, 0:PW] = real
        wt_ref[0:PW, PW:] = -imag
        wt_ref[PW:, 0:PW] = imag
        wt_ref[PW:, PW:] = real
        q_ref[...] = jnp.zeros_like(q_ref)

        def start(b, i):
            degrid_start(
                f_ref, b * capacity + k, table_ref, wt_ref, u_ref.at[i], m_ref.at[i], v_ref.at[i], g_ref.at[i]
            )

        def end(b, i):
            degrid_end(
                f_ref, b * capacity + k, u_ref.at[i], m_ref.at[i], s_ref, v_ref.at[i], g_ref.at[i], q_ref
            )

        start(0, 0)

        def step(j, carry):
            b = 2 * j
            end(b, 0)
            start(b + 1, 1)
            end(b + 1, 1)
            start(jnp.minimum(b + 2, blocks - 1), 0)
            return carry

        lax.fori_loop(0, blocks // 2, step, 0)
        q_re = q_ref[0:PW, 0:PW] + q_ref[PW:, PW:]
        q_im = q_ref[0:PW, PW:] - q_ref[PW:, 0:PW]
        patch_ref[0] = q_re
        patch_ref[1] = q_im
        send_ref[0:PW] = q_re.astype(BF16)
        send_ref[PW : 2 * PW] = q_im.astype(BF16)

    column = jnp.where(k < info_ref[0, capacity], info_ref[0, k], EMPTY)
    send_ref[2 * PW :] = jnp.full((16, PW), column, I32).astype(F32).astype(BF16)


def residual(info, blocks, model_grid, kernels, capacity):
    rows, slots = blocks[0].shape
    patch_rows = model_grid.shape[1]
    whole = lambda shape: pl.BlockSpec(shape, lambda k, i: (0,) * len(shape))
    return pl.pallas_call(
        functools.partial(
            residual_kernel, blocks=len(blocks), capacity=capacity, support=kernels.shape[1] // 4
        ),
        grid_spec=pltpu.PrefetchScalarGridSpec(
            num_scalar_prefetch=1,
            grid=(capacity,),
            in_specs=[whole((rows, slots))] * len(blocks)
            + [
                pl.BlockSpec((2, patch_rows, PW), lambda k, i: (0, 0, jnp.maximum(i[0, k], 0))),
                whole(kernels.shape),
            ],
            out_specs=[
                pl.BlockSpec((None, 2, patch_rows, PW), lambda k, i: (k, 0, 0, 0)),
                pl.BlockSpec((None, 2 * PW + 16, PW), lambda k, i: (k, 0, 0)),
            ],
            scratch_shapes=[
                pltpu.VMEM((len(blocks) * capacity, 8, slots), F32),
                pltpu.VMEM((4, 8, LANES), F32),
                pltpu.VMEM((LANES, LANES), F32),
                pltpu.VMEM((2 * PW, 2 * PW), BF16),
                pltpu.VMEM((2, 2 * PW, slots), BF16),
                pltpu.VMEM((2, 2 * PW, slots), F32),
                pltpu.VMEM((2 * PW, slots), BF16),
                pltpu.VMEM((2, 2, 16, slots), F32),
                pltpu.VMEM((2, 16, slots), I32),
                pltpu.VMEM((2 * PW, 2 * PW), F32),
            ],
        ),
        out_shape=[
            jax.ShapeDtypeStruct((capacity, 2, patch_rows, PW), F32),
            jax.ShapeDtypeStruct((capacity, 2 * PW + 16, PW), BF16),
        ],
        compiler_params=pltpu.CompilerParams(vmem_limit_bytes=VMEM_LIMIT),
        name="degrid_and_grid",
    )(info, *blocks, model_grid, kernels)


def assemble_kernel(info_ref, place_ref, *refs, others, capacity, per_slab, patches):
    received = refs[:others]
    own_ref, out_ref = refs[others:]
    first = place_ref[1] * per_slab + pl.program_id(0) * patches
    out_ref[...] = jnp.zeros_like(out_ref)

    def add(column, real, imag):
        cols = pl.ds(pl.multiple_of((column - first) * PW, PW), PW)
        out_ref[0, :, cols] += real
        out_ref[1, :, cols] += imag

    def add_own(k, carry):
        column = info_ref[0, k]

        @pl.when((k < info_ref[0, capacity]) & (column >= first) & (column < first + patches))
        def _():
            add(column, own_ref[k, 0], own_ref[k, 1])

        return carry

    lax.fori_loop(0, capacity, add_own, 0)
    for ref in received:

        def add_received(k, carry):
            column = jnp.max(ref[k, 2 * PW :].astype(F32)).astype(I32)

            @pl.when((column >= first) & (column < first + patches))
            def _():
                add(column, ref[k, 0:PW].astype(F32), ref[k, PW : 2 * PW].astype(F32))

            return carry

        lax.fori_loop(0, capacity, add_received, 0)


def assemble(info, place, received, own, per_slab):
    capacity, _, patch_rows, _ = own.shape
    patches = min(per_slab, 8)
    whole = lambda shape: pl.BlockSpec(shape, lambda j, i, p: (0,) * len(shape))
    return pl.pallas_call(
        functools.partial(
            assemble_kernel, others=len(received), capacity=capacity, per_slab=per_slab, patches=patches
        ),
        grid_spec=pltpu.PrefetchScalarGridSpec(
            num_scalar_prefetch=2,
            grid=(per_slab // patches,),
            in_specs=[whole(a.shape) for a in (*received, own)],
            out_specs=pl.BlockSpec((2, patch_rows, patches * PW), lambda j, i, p: (0, 0, j)),
        ),
        out_shape=jax.ShapeDtypeStruct((2, patch_rows, per_slab * PW), F32),
        compiler_params=pltpu.CompilerParams(vmem_limit_bytes=VMEM_LIMIT),
        name="assemble_tile",
    )(info, place, *received, own)


def swap(array, axis, distance):
    size = lax.axis_size(axis)
    return lax.ppermute(array, axis, [(i, i ^ distance) for i in range(size)])


def shards(model_grid, kernels, cover, cells, planes, observed, weights):
    tiles = lax.axis_size("grid")
    slabs = lax.axis_size("vis")
    per_tile = model_grid.shape[2] // PW
    per_slab = per_tile // slabs
    capacity = 2 * cover.shape[1] // tiles
    place = jnp.stack([lax.axis_index("grid"), lax.axis_index("vis")]).astype(I32)
    info, *blocks = pack(place, cover, cells, planes, observed, weights, tiles, per_tile, per_slab)
    arrived = [blocks[0], swap(blocks[1], "grid", 1)]
    across = {m: swap(blocks[m ^ 1], "grid", 1) for m in range(2, tiles, 2)}
    for m in range(tiles - 2, 0, -2):
        arrived += [swap(blocks[m], "grid", m), swap(across[m], "grid", m)]
    own, send = residual(info, arrived, model_grid, kernels, capacity)
    received = [swap(send, "vis", v) for v in range(1, slabs)]
    return assemble(info, place, received, own, per_slab)


def solution(mesh):
    placed = (
        P("chan", "grid", None),
        P(),
        P(("chan", "vis"), None),
        P(("chan", "vis"), None, "grid"),
        P(("chan", "vis"), None, "grid"),
        P("chan", "vis", None, "grid"),
        P(("chan", "vis"), None, "grid"),
    )
    return jax.shard_map(
        shards, mesh=mesh, in_specs=placed, out_specs=P("chan", "grid", "vis"), check_vma=False
    )
```

time: 408 us -> 73.5 us (0.18)
  the two profiles are of different devices: /device:TPU:0 before, /device:TPU:24 now
where the time goes in v1:
time: 73.5 us; the launch traced here: 74.2 us
  Pallas kernels  38.9 us (53%)
  waiting for transfers between devices  23.3 us (32%)
  starting transfers between devices  6.94 us (9%)
  local copies, waits for them, and re-layouts  4.98 us (7%)
    pallas_call x1, Pallas kernels, residual(): pl.pallas_call(functools.partial(residual_kernel, blocks=len(blocks), cap...  30.8 us
    ppermute x11, waiting for transfers between devices, swap(): return lax.ppermute(array, axis, [(i, i ^ distance) for i in range(size)])  23.3 us
    ppermute x11, starting transfers between devices, swap(): return lax.ppermute(array, axis, [(i, i ^ distance) for i in range(size)])  6.94 us
    pallas_call x1, Pallas kernels, assemble(): pl.pallas_call(functools.partial(assemble_kernel, others=len(received), c...  6.8 us
    unnamed x12, local copies, waits for them, and re-layouts  4.98 us
  transfers between devices with their start and end apart: 11, of which 5 were waited for; matrix products, arithmetic and copies ran while one was open for 0% of the time, Pallas kernels for 0%

profile of v1, /device:TPU:24, one launch (start us, length us, event | category | flops | bytes accessed | tf_op | source)
XLA Modules:
  0.0 74.2 jit_solution(4807166374702102941)
XLA Ops:
  0.0 0.1 pad_add_fusion.place_ref
  0.1 0.0 copy-start
  0.1 0.9 %copy-done = f32[2,1,32,768]{3,2,1,0:T(8,128)S(1)} copy-done((f32[2,1,32,768]{3,2,1,0:T(8,128)S(1)}, f32[2,1,32,768]{3,2,1,0:T(8,128)}, u32[]{:S(2)}) %copy-start) | copy-done | bytes 196632
  1.0 0.0 copy-start.1
  1.0 0.9 %copy-done.1 = s32[1,32,768]{2,1,0:T(8,128)S(1)} copy-done((s32[1,32,768]{2,1,0:T(8,128)S(1)}, s32[1,32,768]{2,1,0:T(8,128)}, u32[]{:S(2)}) %copy-start.1) | copy-done | bytes 98328
  1.9 0.0 copy-start.2
  1.9 0.9 %copy-done.2 = s32[1,32,768]{2,1,0:T(8,128)S(1)} copy-done((s32[1,32,768]{2,1,0:T(8,128)S(1)}, s32[1,32,768]{2,1,0:T(8,128)}, u32[]{:S(2)}) %copy-start.2) | copy-done | bytes 98328
  2.8 0.0 copy-start.3
  2.8 0.9 %copy-done.3 = f32[1,32,768]{2,1,0:T(8,128)S(1)} copy-done((f32[1,32,768]{2,1,0:T(8,128)S(1)}, f32[1,32,768]{2,1,0:T(8,128)}, u32[]{:S(2)}) %copy-start.3) | copy-done | bytes 98328
  3.7 0.0 copy-start.5
  3.7 0.7 copy-done.5
  4.3 1.3 %pack_by_tile.1 = (s32[8,128]{1,0:T(8,128)S(1)}, bf16[48,768]{1,0:T(8,128)(2,1)S(1)}, bf16[48,768]{1,0:T(8,128)(2,1)S(1)}, bf16[48,768]{1,0:T(8,128)(2,1)S(1)}, ...) custom-call(s32[2]{0:T(128)S(1)} %pad_add_fusion.place_ref, ...), custom_call_target="tpu_custom_call" | custom-call | tf_op jit(solution)/shard_map/pack_by_tile/pallas_call | solution.py:96
  5.6 0.1 collective-permute-start
  5.7 0.1 collective-permute-start.1
  5.8 0.4 collective-permute-start.2
  6.2 0.2 collective-permute-start.5
  6.4 0.4 collective-permute-start.8
  6.7 0.2 collective-permute-done.refs_1_
  7.0 1.4 %collective-permute-start.4 = (bf16[48,768]{1,0:T(8,128)(2,1)S(1)}, bf16[48,768]{1,0:T(8,128)(2,1)S(1)}, u32[]{:S(2)}, u32[]{:S(2)}) collective-permute-start(bf16[48,768]{1,0:T(8,128)(2,1)S(1)} %get-tuple-element.21), channel_id=1, source_target_pairs={{0,8},{2,10},{4,12},{6,14},{8,0},{10,2},{12,4},{14,6},{1,9},{3,11}... | collective-permute-start | bytes 221192 | tf_op jit(solution)/shard_map/ppermute | solution.py:346
  8.4 4.4 %collective-permute-done.1.refs_2_ = bf16[48,768]{1,0:T(8,128)(2,1)S(1)} collective-permute-done((bf16[48,768]{1,0:T(8,128)(2,1)S(1)}, bf16[48,768]{1,0:T(8,128)(2,1)S(1)}, u32[]{:S(2)}, u32[]{:S(2)}) %collective-permute-start.1) | collective-permute-done | bytes 73760 | tf_op jit(solution)/shard_map/ppermute | solution.py:346
  12.7 0.0 collective-permute-start.7
  12.8 0.0 collective-permute-done.2
  12.8 1.0 %collective-permute-start.3 = (bf16[48,768]{1,0:T(8,128)(2,1)S(1)}, bf16[48,768]{1,0:T(8,128)(2,1)S(1)}, u32[]{:S(2)}, u32[]{:S(2)}) collective-permute-start(bf16[48,768]{1,0:T(8,128)(2,1)S(1)} %collective-permute-done.2), channel_id=1, source_target_pairs={{0,12},{2,14},{4,8},{6,10},{8,4},{10,6},{12,0},{14,2},{1,13},{3,15... | collective-permute-start | bytes 221192 | tf_op jit(solution)/shard_map/ppermute | solution.py:346
  13.8 0.0 collective-permute-done.5
  13.8 2.4 %collective-permute-start.6 = (bf16[48,768]{1,0:T(8,128)(2,1)S(1)}, bf16[48,768]{1,0:T(8,128)(2,1)S(1)}, u32[]{:S(2)}, u32[]{:S(2)}) collective-permute-start(bf16[48,768]{1,0:T(8,128)(2,1)S(1)} %collective-permute-done.5), channel_id=1, source_target_pairs={{0,8},{2,10},{4,12},{6,14},{8,0},{10,2},{12,4},{14,6},{1,9},{3,11}... | collective-permute-start | bytes 221192 | tf_op jit(solution)/shard_map/ppermute | solution.py:346
  16.2 0.0 collective-permute-done.8
  16.2 0.9 %collective-permute-start.9 = (bf16[48,768]{1,0:T(8,128)(2,1)S(1)}, bf16[48,768]{1,0:T(8,128)(2,1)S(1)}, u32[]{:S(2)}, u32[]{:S(2)}) collective-permute-start(bf16[48,768]{1,0:T(8,128)(2,1)S(1)} %collective-permute-done.8), channel_id=1, source_target_pairs={{0,4},{2,6},{4,0},{6,2},{8,12},{10,14},{12,8},{14,10},{1,5},{3,7},... | collective-permute-start | bytes 221192 | tf_op jit(solution)/shard_map/ppermute | solution.py:346
  17.2 0.0 collective-permute-done.4.refs_4_
  17.2 2.5 %collective-permute-done.7.refs_6_ = bf16[48,768]{1,0:T(8,128)(2,1)S(1)} collective-permute-done((bf16[48,768]{1,0:T(8,128)(2,1)S(1)}, bf16[48,768]{1,0:T(8,128)(2,1)S(1)}, u32[]{:S(2)}, u32[]{:S(2)}) %collective-permute-start.7) | collective-permute-done | bytes 73760 | tf_op jit(solution)/shard_map/ppermute | solution.py:346
  19.6 0.0 collective-permute-done.3.refs_3_
  19.6 2.3 %collective-permute-done.6.refs_5_ = bf16[48,768]{1,0:T(8,128)(2,1)S(1)} collective-permute-done((bf16[48,768]{1,0:T(8,128)(2,1)S(1)}, bf16[48,768]{1,0:T(8,128)(2,1)S(1)}, u32[]{:S(2)}, u32[]{:S(2)}) %collective-permute-start.6) | collective-permute-done | bytes 73760 | tf_op jit(solution)/shard_map/ppermute | solution.py:346
  22.0 0.0 collective-permute-done.9.refs_7_
  22.0 0.0 copy-start.4
  22.0 0.7 copy-done.4
  22.7 30.8 %degrid_and_grid.1 = (f32[8,2,128,128]{3,2,1,0:T(8,128)S(1)}, bf16[8,272,128]{2,1,0:T(8,128)(2,1)S(1)}) custom-call(s32[8,128]{1,0:T(8,128)S(1)} %get-tuple-element.16.info_ref, bf16[48,768]{1,0:T(8,128)(2,1)S(1)} %get-tuple-element.17.refs_0_, bf16[48,768]{1,0:T(8,128)(2,1)S(1)} %collective-permute-done.refs_1_, ...), custom_call_target="tpu_custom_call" | custom-call | tf_op jit(solution)/shard_map/degrid_and_grid/pallas_call | solution.py:251
  53.5 0.1 collective-permute-start.10
  53.6 13.8 %collective-permute-done.10.refs_0_ = bf16[8,272,128]{2,1,0:T(8,128)(2,1)S(1)} collective-permute-done((bf16[8,272,128]{2,1,0:T(8,128)(2,1)S(1)}, bf16[8,272,128]{2,1,0:T(8,128)(2,1)S(1)}, u32[]{:S(2)}, u32[]{:S(2)}) %collective-permute-start.10) | collective-permute-done | bytes 557088 | tf_op jit(solution)/shard_map/ppermute | solution.py:346
  67.4 6.8 %assemble_tile.1 = f32[2,128,4096]{2,1,0:T(8,128)} custom-call(s32[8,128]{1,0:T(8,128)S(1)} %get-tuple-element.16.info_ref, s32[2]{0:T(128)S(1)} %pad_add_fusion.place_ref, bf16[8,272,128]{2,1,0:T(8,128)(2,1)S(1)} %collective-permute-done.10.refs_0_, f32[8,2,128,128]{3,2,1,0:T(8,128)S(1)} %get-tuple-element.26.refs_1_), custom_call_target="tpu_custom_call" | custom-call | tf_op jit(solution)/shard_map/assemble_tile/pallas_call | solution.py:328
Async XLA Ops:
  0.1 0.9 %copy-start = (f32[2,1,32,768]{3,2,1,0:T(8,128)S(1)}, f32[2,1,32,768]{3,2,1,0:T(8,128)}, u32[]{:S(2)}) copy-start(f32[2,1,32,768]{3,2,1,0:T(8,128)} %observed_ref.1) | copy-start | bytes 589828
  1.0 0.9 %copy-start.1 = (s32[1,32,768]{2,1,0:T(8,128)S(1)}, s32[1,32,768]{2,1,0:T(8,128)}, u32[]{:S(2)}) copy-start(s32[1,32,768]{2,1,0:T(8,128)} %cells_ref.1) | copy-start | bytes 294916
  1.9 0.9 %copy-start.2 = (s32[1,32,768]{2,1,0:T(8,128)S(1)}, s32[1,32,768]{2,1,0:T(8,128)}, u32[]{:S(2)}) copy-start(s32[1,32,768]{2,1,0:T(8,128)} %planes_ref.1) | copy-start | bytes 294916
  2.8 0.9 %copy-start.3 = (f32[1,32,768]{2,1,0:T(8,128)S(1)}, f32[1,32,768]{2,1,0:T(8,128)}, u32[]{:S(2)}) copy-start(f32[1,32,768]{2,1,0:T(8,128)} %weights_ref.1) | copy-start | bytes 294916
  3.7 0.7 copy-start.5
  5.6 1.3 %collective-permute-start = (bf16[48,768]{1,0:T(8,128)(2,1)S(1)}, bf16[48,768]{1,0:T(8,128)(2,1)S(1)}, u32[]{:S(2)}, u32[]{:S(2)}) collective-permute-start(bf16[48,768]{1,0:T(8,128)(2,1)S(1)} %get-tuple-element.18), channel_id=1, source_target_pairs={{0,2},{2,0},{4,6},{6,4},{8,10},{10,8},{12,14},{14,12},{1,3},{3,1},... | collective-permute-start | bytes 221192 | tf_op jit(solution)/shard_map/ppermute | solution.py:346
  5.7 7.0 %collective-permute-start.1 = (bf16[48,768]{1,0:T(8,128)(2,1)S(1)}, bf16[48,768]{1,0:T(8,128)(2,1)S(1)}, u32[]{:S(2)}, u32[]{:S(2)}) collective-permute-start(bf16[48,768]{1,0:T(8,128)(2,1)S(1)} %get-tuple-element.19), channel_id=1, source_target_pairs={{0,12},{2,14},{4,8},{6,10},{8,4},{10,6},{12,0},{14,2},{1,13},{3,15... | collective-permute-start | bytes 221192 | tf_op jit(solution)/shard_map/ppermute | solution.py:346
  5.8 7.0 %collective-permute-start.2 = (bf16[48,768]{1,0:T(8,128)(2,1)S(1)}, bf16[48,768]{1,0:T(8,128)(2,1)S(1)}, u32[]{:S(2)}, u32[]{:S(2)}) collective-permute-start(bf16[48,768]{1,0:T(8,128)(2,1)S(1)} %get-tuple-element.20), channel_id=1, source_target_pairs={{0,2},{2,0},{4,6},{6,4},{8,10},{10,8},{12,14},{14,12},{1,3},{3,1},... | collective-permute-start | bytes 221192 | tf_op jit(solution)/shard_map/ppermute | solution.py:346
  6.2 7.6 %collective-permute-start.5 = (bf16[48,768]{1,0:T(8,128)(2,1)S(1)}, bf16[48,768]{1,0:T(8,128)(2,1)S(1)}, u32[]{:S(2)}, u32[]{:S(2)}) collective-permute-start(bf16[48,768]{1,0:T(8,128)(2,1)S(1)} %get-tuple-element.22), channel_id=1, source_target_pairs={{0,2},{2,0},{4,6},{6,4},{8,10},{10,8},{12,14},{14,12},{1,3},{3,1},... | collective-permute-start | bytes 221192 | tf_op jit(solution)/shard_map/ppermute | solution.py:346
  6.4 9.9 %collective-permute-start.8 = (bf16[48,768]{1,0:T(8,128)(2,1)S(1)}, bf16[48,768]{1,0:T(8,128)(2,1)S(1)}, u32[]{:S(2)}, u32[]{:S(2)}) collective-permute-start(bf16[48,768]{1,0:T(8,128)(2,1)S(1)} %get-tuple-element.24), channel_id=1, source_target_pairs={{0,2},{2,0},{4,6},{6,4},{8,10},{10,8},{12,14},{14,12},{1,3},{3,1},... | collective-permute-start | bytes 221192 | tf_op jit(solution)/shard_map/ppermute | solution.py:346
  7.0 10.2 %collective-permute-start.4 = (bf16[48,768]{1,0:T(8,128)(2,1)S(1)}, bf16[48,768]{1,0:T(8,128)(2,1)S(1)}, u32[]{:S(2)}, u32[]{:S(2)}) collective-permute-start(bf16[48,768]{1,0:T(8,128)(2,1)S(1)} %get-tuple-element.21), channel_id=1, source_target_pairs={{0,8},{2,10},{4,12},{6,14},{8,0},{10,2},{12,4},{14,6},{1,9},{3,11}... | collective-permute-start | bytes 221192 | tf_op jit(solution)/shard_map/ppermute | solution.py:346
  12.7 6.9 %collective-permute-start.7 = (bf16[48,768]{1,0:T(8,128)(2,1)S(1)}, bf16[48,768]{1,0:T(8,128)(2,1)S(1)}, u32[]{:S(2)}, u32[]{:S(2)}) collective-permute-start(bf16[48,768]{1,0:T(8,128)(2,1)S(1)} %get-tuple-element.23), channel_id=1, source_target_pairs={{0,4},{2,6},{4,0},{6,2},{8,12},{10,14},{12,8},{14,10},{1,5},{3,7},... | collective-permute-start | bytes 221192 | tf_op jit(solution)/shard_map/ppermute | solution.py:346
  12.8 6.9 %collective-permute-start.3 = (bf16[48,768]{1,0:T(8,128)(2,1)S(1)}, bf16[48,768]{1,0:T(8,128)(2,1)S(1)}, u32[]{:S(2)}, u32[]{:S(2)}) collective-permute-start(bf16[48,768]{1,0:T(8,128)(2,1)S(1)} %collective-permute-done.2), channel_id=1, source_target_pairs={{0,12},{2,14},{4,8},{6,10},{8,4},{10,6},{12,0},{14,2},{1,13},{3,15... | collective-permute-start | bytes 221192 | tf_op jit(solution)/shard_map/ppermute | solution.py:346
  13.8 8.2 %collective-permute-start.6 = (bf16[48,768]{1,0:T(8,128)(2,1)S(1)}, bf16[48,768]{1,0:T(8,128)(2,1)S(1)}, u32[]{:S(2)}, u32[]{:S(2)}) collective-permute-start(bf16[48,768]{1,0:T(8,128)(2,1)S(1)} %collective-permute-done.5), channel_id=1, source_target_pairs={{0,8},{2,10},{4,12},{6,14},{8,0},{10,2},{12,4},{14,6},{1,9},{3,11}... | collective-permute-start | bytes 221192 | tf_op jit(solution)/shard_map/ppermute | solution.py:346
  16.2 5.7 %collective-permute-start.9 = (bf16[48,768]{1,0:T(8,128)(2,1)S(1)}, bf16[48,768]{1,0:T(8,128)(2,1)S(1)}, u32[]{:S(2)}, u32[]{:S(2)}) collective-permute-start(bf16[48,768]{1,0:T(8,128)(2,1)S(1)} %collective-permute-done.8), channel_id=1, source_target_pairs={{0,4},{2,6},{4,0},{6,2},{8,12},{10,14},{12,8},{14,10},{1,5},{3,7},... | collective-permute-start | bytes 221192 | tf_op jit(solution)/shard_map/ppermute | solution.py:346
  22.0 0.7 copy-start.4
  53.5 13.9 %collective-permute-start.10 = (bf16[8,272,128]{2,1,0:T(8,128)(2,1)S(1)}, bf16[8,272,128]{2,1,0:T(8,128)(2,1)S(1)}, u32[]{:S(2)}, u32[]{:S(2)}) collective-permute-start(bf16[8,272,128]{2,1,0:T(8,128)(2,1)S(1)} %get-tuple-element.25), channel_id=1, source_target_pairs={{0,1},{1,0},{2,3},{3,2},{4,5},{5,4},{6,7},{7,6},{8,9},{9,8},{10,11... | collective-permute-start | bytes 1671176 | tf_op jit(solution)/shard_map/ppermute | solution.py:346

commit v2 on v1

v2 whole, which is shorter than its diff:
```python
import functools

import jax
import jax.numpy as jnp
from jax import lax
from jax.experimental import pallas as pl
from jax.experimental.pallas import tpu as pltpu
from jax.sharding import PartitionSpec as P

PW = 128
LANES = 128
FIELDS = 6
BF16 = jnp.bfloat16
F32 = jnp.float32
I32 = jnp.int32
VMEM_LIMIT = 48 * 1024 * 1024
EMPTY = 255


def round_up(value, unit):
    return -(-value // unit) * unit


def whole_block(shape):
    return pl.BlockSpec(shape, lambda *_: (0,) * len(shape))


def iota(shape, dim):
    return lax.broadcasted_iota(I32, shape, dim)


def pack_kernel(
    place_ref, cover_hbm, cells_hbm, planes_hbm, observed_hbm, weights_hbm, info_ref, *refs,
    count, tiles, per_tile, per_slab, capacity, rows,
):
    outs = refs[: tiles // 2]
    cover_ref, cells_ref, planes_ref, observed_ref, weights_ref, sem = refs[tiles // 2 :]
    sources = (cover_hbm, cells_hbm, planes_hbm, observed_hbm, weights_hbm)
    targets = (cover_ref, cells_ref, planes_ref, observed_ref, weights_ref)
    copies = [pltpu.make_async_copy(x, y, sem.at[i]) for i, (x, y) in enumerate(zip(sources, targets))]
    for copy in copies:
        copy.start()
    me = place_ref[0]
    slab = place_ref[1]
    copies[0].wait()
    cover_row = cover_ref[...]
    across = jnp.broadcast_to(cover_row, (count, count))
    left = iota((count, count), 0)
    right = iota((count, count), 1)
    cover_col = jnp.sum(jnp.where(left == right, across, 0), axis=1, keepdims=True)

    def order_key(patch, entry):
        owner = patch // per_tile
        foreign = jnp.where((patch - owner * per_tile) // per_slab == slab, 1, 0)
        return owner, foreign * count + entry

    owner_i, key_i = order_key(cover_col, iota((count, 1), 0))
    owner_j, key_j = order_key(cover_row, iota((1, count), 1))
    same = owner_i == owner_j
    rank_row = jnp.sum(jnp.where(same & (key_i < key_j), 1, 0), axis=0, keepdims=True)
    rank_col = jnp.sum(jnp.where(same & (key_j < key_i), 1, 0), axis=1, keepdims=True)

    slot = iota((count, LANES), 1)
    own = (owner_i == me) & (rank_col == slot)
    column = cover_col - owner_i * per_tile
    listed = jnp.sum(jnp.where(own, column + 1, 0), axis=0, keepdims=True)
    total = jnp.sum(jnp.where(owner_i == me, 1, 0), axis=0, keepdims=True)
    lane = iota((1, LANES), 1)
    info = jnp.where(lane < capacity, listed - 1, jnp.where(lane == capacity, total, 0))
    info_ref[...] = jnp.broadcast_to(info, info_ref.shape)

    route = (owner_j ^ me) * capacity + rank_row
    spread = (iota((count, FIELDS * count), 1) % count == iota((count, FIELDS * count), 0)).astype(F32)
    wide = jnp.dot(
        jnp.broadcast_to(route.astype(F32), (8, count)).astype(BF16), spread.astype(BF16),
        preferred_element_type=F32,
    )[0:1].astype(I32)
    field_j = iota((1, FIELDS * count), 1) // count
    for copy in copies[1:]:
        copy.wait()
    cells = cells_ref[0]
    row_off = cells // PW
    fields = [row_off, cells - row_off * PW, planes_ref[0], observed_ref[0, 0], observed_ref[1, 0], weights_ref[0]]
    data = jnp.concatenate([field.astype(F32).astype(BF16) for field in fields], axis=0)
    line = iota((rows, FIELDS * count), 0)
    for m in range(tiles):
        field_i = line // capacity
        pick = (field_i == field_j) & (wide == m * capacity + line - field_i * capacity)
        block = jnp.dot(pick.astype(F32).astype(BF16), data, preferred_element_type=F32)
        outs[m // 2][rows * (m % 2) : rows * (m % 2 + 1)] = block.astype(BF16)


def in_hbm(array):
    return pltpu.with_memory_space_constraint(array, pltpu.HBM)


def pack(place, cover, cells, planes, observed, weights, tiles, per_tile, per_slab):
    count, slots = cells.shape[1:]
    capacity = 2 * count // tiles
    rows = round_up(FIELDS * capacity, 16)
    arrays = (cover, cells, planes, observed, weights)
    outputs = [((8, LANES), I32)] + [((2 * rows, slots), BF16)] * (tiles // 2)
    return pl.pallas_call(
        functools.partial(
            pack_kernel, count=count, tiles=tiles, per_tile=per_tile, per_slab=per_slab,
            capacity=capacity, rows=rows,
        ),
        grid_spec=pltpu.PrefetchScalarGridSpec(
            num_scalar_prefetch=1,
            grid=(1,),
            in_specs=[pl.BlockSpec(memory_space=pltpu.HBM)] * len(arrays),
            out_specs=[whole_block(shape) for shape, _ in outputs],
            scratch_shapes=[pltpu.VMEM(a.shape, a.dtype) for a in arrays]
            + [pltpu.SemaphoreType.DMA((len(arrays),))],
        ),
        out_shape=[jax.ShapeDtypeStruct(shape, dtype) for shape, dtype in outputs],
        compiler_params=pltpu.CompilerParams(vmem_limit_bytes=VMEM_LIMIT),
        name="pack_by_tile",
    )(place, *[in_hbm(a) for a in arrays])


def fill_tables(kern_ref, wide_ref, table_ref, support):
    wide_ref[...] = jnp.zeros_like(wide_ref)
    wide_ref[0 : kern_ref.shape[0], 0 : kern_ref.shape[1]] = kern_ref[...]
    flipped = wide_ref[...].T
    zero = jnp.zeros((8 - support, LANES), F32)
    for group in range(4):
        taps = flipped[support * group : support * (group + 1)]
        table_ref[group] = jnp.concatenate([taps, zero], axis=0)


def pick(array, index, axis):
    return jnp.take_along_axis(array, index, axis=axis)


def tap_places(offset):
    wide = jnp.broadcast_to(offset, (16, LANES))
    s = iota((16, LANES), 0)
    return jnp.minimum((s - wide) & 15, 7), (wide + 15 - s) >> 4


def wrapped(taps, places):
    return jnp.concatenate([pick(taps, places[0:8], 0), pick(taps, places[8:16], 0)], axis=0)


def expand(ref, base, cols, rows, group):
    group = group.astype(F32).astype(BF16)
    for q in range(PW // 16):
        ref[base + 16 * q : base + 16 * q + 16, cols] = jnp.where(group == BF16(q), rows, BF16(0))


def degrid_start(f_ref, item, table_ref, wt_ref, u_ref, m_ref, v_ref, g_ref):
    for t in range(u_ref.shape[1] // LANES):
        cols = pl.ds(t * LANES, LANES)
        row_off = f_ref[item, 0:1, cols].astype(I32)
        col_off = f_ref[item, 1:2, cols].astype(I32)
        plane = jnp.broadcast_to(f_ref[item, 2:3, cols].astype(I32), (8, LANES))
        u_place, u_group = tap_places(row_off)
        v_place, v_group = tap_places(col_off)
        u_re = wrapped(pick(table_ref[0], plane, 1), u_place).astype(BF16)
        u_im = wrapped(pick(table_ref[1], plane, 1), u_place).astype(BF16)
        v_ref[0, :, cols] = wrapped(pick(table_ref[2], plane, 1), v_place)
        v_ref[1, :, cols] = wrapped(pick(table_ref[3], plane, 1), v_place)
        g_ref[:, cols] = v_group
        expand(u_ref, 0, cols, u_re, u_group)
        expand(u_ref, PW, cols, u_im, u_group)
    m_ref[...] = jnp.dot(wt_ref[...], u_ref[...], preferred_element_type=F32)


def degrid_end(f_ref, item, u_ref, m_ref, s_ref, v_ref, g_ref, q_ref):
    for t in range(u_ref.shape[1] // LANES):
        cols = pl.ds(t * LANES, LANES)
        group = g_ref[:, cols]
        m_re = jnp.zeros((16, LANES), F32)
        m_im = jnp.zeros((16, LANES), F32)
        for q in range(PW // 16):
            hit = group == q
            m_re = jnp.where(hit, m_ref[16 * q : 16 * q + 16, cols], m_re)
            m_im = jnp.where(hit, m_ref[PW + 16 * q : PW + 16 * q + 16, cols], m_im)
        v_re = v_ref[0, :, cols]
        v_im = v_ref[1, :, cols]
        model_re = jnp.sum(m_re * v_re - m_im * v_im, axis=0, keepdims=True)
        model_im = jnp.sum(m_re * v_im + m_im * v_re, axis=0, keepdims=True)
        weight = f_ref[item, 5:6, cols]
        res_re = weight * (f_ref[item, 3:4, cols] - model_re)
        res_im = weight * (f_ref[item, 4:5, cols] - model_im)
        s_re = (res_re * v_re + res_im * v_im).astype(BF16)
        s_im = (res_im * v_re - res_re * v_im).astype(BF16)
        expand(s_ref, 0, cols, s_re, group)
        expand(s_ref, PW, cols, s_im, group)
    q_ref[...] += lax.dot_general(
        u_ref[...], s_ref[...], (((1,), (1,)), ((), ())), preferred_element_type=F32
    )


def residual_kernel(info_ref, *refs, sources, capacity, first, final, resumed, zeros, support):
    refs = list(refs)
    take = lambda number: [refs.pop(0) for _ in range(number)]
    block_refs = take(sources)
    model_ref, kern_ref = take(2)
    before_ref = take(1)[0] if resumed else None
    patch_ref = take(1)[0]
    send_ref = take(1)[0] if final else None
    tile_ref = take(1)[0] if zeros else None
    f_ref, table_ref, wide_ref, wt_ref, wt_next_ref, s_ref, q_ref = take(7)
    u, m, v, g = (take(sources) for _ in range(4))
    step = pl.program_id(0)
    steps = pl.num_programs(0)
    k = first + step - 1
    total = info_ref[0, capacity]
    if zeros:
        zero_ref, sem = take(2)
        width = zero_ref.shape[2]
        clears = [
            pltpu.make_async_copy(zero_ref, tile_ref.at[:, :, pl.ds(i * width, width)], sem.at[i])
            for i in range(zeros)
        ]

    def turn(model, target):
        real = model[0].T
        imag = model[1].T
        target[0:PW, 0:PW] = real
        target[0:PW, PW:] = -imag
        target[PW:, 0:PW] = imag
        target[PW:, PW:] = real

    def start(slot, b, w):
        degrid_start(f_ref, b * capacity + slot, table_ref, w, u[b], m[b], v[b], g[b])

    def end(slot, b):
        degrid_end(f_ref, b * capacity + slot, u[b], m[b], s_ref, v[b], g[b], q_ref)

    @pl.when(step == 0)
    def _():
        if zeros:
            zero_ref[...] = jnp.zeros_like(zero_ref)
            for copy in clears:
                copy.start()
        fill_tables(kern_ref, wide_ref, table_ref, support)
        shape = (8 * capacity, block_refs[0].shape[0])
        line = iota(shape, 0)
        order = (iota(shape, 1) == (line & 7) * capacity + (line >> 3)).astype(F32).astype(BF16)
        for b in range(sources):
            fields = jnp.dot(order, block_refs[b][...], preferred_element_type=F32)
            for slot in range(capacity):
                f_ref[b * capacity + slot] = fields[8 * slot : 8 * slot + 8]
        turn(model_ref, wt_ref)
        start(first, 0, wt_ref)

    @pl.when((step > 0) & (k < total))
    def _():
        turn(model_ref, wt_next_ref)
        q_ref[...] = jnp.zeros_like(q_ref)
        for b in range(sources):
            end(k, b)
            if b + 1 < sources:
                start(k, b + 1, wt_ref)
            else:
                start(jnp.minimum(k + 1, capacity - 1), 0, wt_next_ref)
        wt_ref[...] = wt_next_ref[...]
        q_re = q_ref[0:PW, 0:PW] + q_ref[PW:, PW:]
        q_im = q_ref[0:PW, PW:] - q_ref[PW:, 0:PW]
        if resumed:
            q_re += before_ref[0]
            q_im += before_ref[1]
        patch_ref[0] = q_re
        patch_ref[1] = q_im
        if final:
            send_ref[0:PW] = q_re.astype(BF16)
            send_ref[PW : 2 * PW] = q_im.astype(BF16)

    if final:
        column = jnp.where(k < total, info_ref[0, jnp.maximum(k, 0)], EMPTY)
        send_ref[2 * PW :] = jnp.full((16, PW), column, I32).astype(F32).astype(BF16)
    if zeros:

        @pl.when(step == steps - 1)
        def _():
            for copy in clears:
                copy.wait()


def residual(info, sources, model_grid, kernels, capacity, first, steps, before=None, final=False, tile_columns=0):
    rows, slots = sources[0][0].shape
    rows //= 2
    patch_rows = model_grid.shape[1]
    number = len(sources)
    patch_block = (None, 2, patch_rows, PW)
    in_specs = [pl.BlockSpec((rows, slots), lambda s, i, half=half: (half, 0)) for _, half in sources]
    in_specs += [
        pl.BlockSpec(
            (2, patch_rows, PW), lambda s, i: (0, 0, jnp.maximum(i[0, jnp.minimum(first + s, capacity - 1)], 0))
        ),
        whole_block(kernels.shape),
    ]
    operands = [array for array, _ in sources] + [in_hbm(model_grid), in_hbm(kernels)]
    if before is not None:
        in_specs.append(pl.BlockSpec(patch_block, lambda s, i: (first + jnp.maximum(s - 1, 0), 0, 0, 0)))
        operands.append(before)
    out_specs = [pl.BlockSpec(patch_block, lambda s, i: (jnp.maximum(s - 1, 0), 0, 0, 0))]
    out_shape = [jax.ShapeDtypeStruct((steps, 2, patch_rows, PW), F32)]
    scratch = [
        pltpu.VMEM((number * capacity, 8, slots), F32),
        pltpu.VMEM((4, 8, LANES), F32),
        pltpu.VMEM((LANES, LANES), F32),
        pltpu.VMEM((2 * PW, 2 * PW), BF16),
        pltpu.VMEM((2 * PW, 2 * PW), BF16),
        pltpu.VMEM((2 * PW, slots), BF16),
        pltpu.VMEM((2 * PW, 2 * PW), F32),
    ]
    scratch += [pltpu.VMEM((2 * PW, slots), BF16)] * number
    scratch += [pltpu.VMEM((2 * PW, slots), F32)] * number
    scratch += [pltpu.VMEM((2, 16, slots), F32)] * number
    scratch += [pltpu.VMEM((16, slots), I32)] * number
    if final:
        out_specs.append(pl.BlockSpec((None, 2 * PW + 16, PW), lambda s, i: (jnp.maximum(s - 1, 0), 0, 0)))
        out_shape.append(jax.ShapeDtypeStruct((steps, 2 * PW + 16, PW), BF16))
    zeros = 0
    if tile_columns:
        width = min(tile_columns, 4 * PW)
        zeros = tile_columns // width
        out_specs.append(pl.BlockSpec(memory_space=pltpu.HBM))
        out_shape.append(jax.ShapeDtypeStruct((2, patch_rows, tile_columns), F32))
        scratch += [pltpu.VMEM((2, patch_rows, width), F32), pltpu.SemaphoreType.DMA((zeros,))]
    return pl.pallas_call(
        functools.partial(
            residual_kernel, sources=number, capacity=capacity, first=first, final=final,
            resumed=before is not None, zeros=zeros, support=kernels.shape[1] // 4,
        ),
        grid_spec=pltpu.PrefetchScalarGridSpec(
            num_scalar_prefetch=1, grid=(steps + 1,), in_specs=in_specs, out_specs=out_specs, scratch_shapes=scratch
        ),
        out_shape=out_shape,
        compiler_params=pltpu.CompilerParams(vmem_limit_bytes=VMEM_LIMIT),
        cost_estimate=pl.CostEstimate(
            flops=steps * number * slots * 16 * PW * PW, bytes_accessed=steps * 65536, transcendentals=0
        ),
        name="degrid_and_grid",
    )(info, *operands)


def place_own_kernel(info_ref, place_ref, *refs, groups, capacity, per_slab):
    own_refs = refs[:groups]
    tile_ref, sem = refs[groups + 1 :]
    slab_start = place_ref[1] * per_slab
    total = info_ref[0, capacity]
    slots = [ref.at[k] for ref in own_refs for k in range(ref.shape[0])]

    def each(act):
        for k in range(capacity):
            local = info_ref[0, k] - slab_start

            @pl.when((k < total) & (local >= 0) & (local < per_slab))
            def _():
                cols = pl.ds(pl.multiple_of(local * PW, PW), PW)
                act(pltpu.make_async_copy(slots[k], tile_ref.at[:, :, cols], sem.at[k]))

    each(lambda copy: copy.start())
    each(lambda copy: copy.wait())


def place_received_kernel(info_ref, place_ref, received_ref, *refs, groups, capacity, per_slab, reread):
    own_refs = refs[:groups]
    tile_ref, sum_ref, sem = refs[groups + 1 :]
    slab_start = place_ref[1] * per_slab
    total = info_ref[0, capacity]
    slots = [ref.at[k] for ref in own_refs for k in range(ref.shape[0])]
    number = received_ref.shape[0]
    columns = [jnp.max(received_ref[k, 2 * PW :].astype(F32)).astype(I32) for k in range(number)]

    def each(act):
        for k in range(number):
            local = columns[k] - slab_start

            @pl.when((local >= 0) & (local < per_slab))
            def _():
                cols = pl.ds(pl.multiple_of(local * PW, PW), PW)
                act(k, pltpu.make_async_copy(sum_ref.at[k], tile_ref.at[:, :, cols], sem.at[k]))

    def send(k, copy):
        if reread:
            cols = pl.ds(pl.multiple_of((columns[k] - slab_start) * PW, PW), PW)
            there = pltpu.make_async_copy(tile_ref.at[:, :, cols], sum_ref.at[k], sem.at[k])
            there.start()
            there.wait()
            sum_ref[k, 0] += received_ref[k, 0:PW].astype(F32)
            sum_ref[k, 1] += received_ref[k, PW : 2 * PW].astype(F32)
            copy.start()
            return
        sum_ref[k, 0] = received_ref[k, 0:PW].astype(F32)
        sum_ref[k, 1] = received_ref[k, PW : 2 * PW].astype(F32)
        for j in range(capacity):

            @pl.when((j < total) & (info_ref[0, j] == columns[k]))
            def _():
                sum_ref[k] += slots[j][...]

        copy.start()

    each(send)
    each(lambda k, copy: copy.wait())


def place_patches(kernel, info, place, received, own, tile, per_slab, reread=False):
    groups = len(own)
    capacity = sum(patches.shape[0] for patches in own)
    scratch = [pltpu.SemaphoreType.DMA((capacity,))]
    if received:
        number, _, width = received[0].shape
        scratch = [pltpu.VMEM((number, 2, tile.shape[1], PW), F32), pltpu.SemaphoreType.DMA((number,))]
        kernel = functools.partial(kernel, reread=reread)
    operands = [*received, *own]
    return pl.pallas_call(
        functools.partial(kernel, groups=groups, capacity=capacity, per_slab=per_slab),
        grid_spec=pltpu.PrefetchScalarGridSpec(
            num_scalar_prefetch=2,
            grid=(1,),
            in_specs=[whole_block(a.shape) for a in operands] + [pl.BlockSpec(memory_space=pltpu.HBM)],
            out_specs=pl.BlockSpec(memory_space=pltpu.HBM),
            scratch_shapes=scratch,
        ),
        out_shape=jax.ShapeDtypeStruct(tile.shape, tile.dtype),
        input_output_aliases={2 + len(operands): 0},
        compiler_params=pltpu.CompilerParams(vmem_limit_bytes=VMEM_LIMIT),
        name="place_received" if received else "place_own",
    )(info, place, *operands, tile)


def swap(array, axis, distance):
    size = lax.axis_size(axis)
    return lax.ppermute(array, axis, [(i, i ^ distance) for i in range(size)])


def shards(model_grid, kernels, cover, cells, planes, observed, weights):
    tiles = lax.axis_size("grid")
    slabs = lax.axis_size("vis")
    per_tile = model_grid.shape[2] // PW
    per_slab = per_tile // slabs
    capacity = 2 * cover.shape[1] // tiles
    place = jnp.stack([lax.axis_index("grid"), lax.axis_index("vis")]).astype(I32)
    info, *pairs = pack(place, cover, cells, planes, observed, weights, tiles, per_tile, per_slab)
    arrived = [pairs[0]] + [swap(pairs[i], "grid", 2 * i) for i in range(1, tiles // 2)]
    run = functools.partial(residual, info, model_grid=model_grid, kernels=kernels, capacity=capacity)
    both = lambda pair: ((pair, 0), (swap(pair, "grid", 1), 1))
    before, tile = run(sources=both(arrived[0]), first=0, steps=capacity, tile_columns=per_slab * PW)
    before, *arrived[1:] = lax.optimization_barrier((before, *arrived[1:]))
    sources = [both(pair) for pair in arrived[1:]]
    while len(sources) > 3:
        (before,) = run(sources=sources.pop(0), first=0, steps=capacity, before=before)
    sources = sum(sources, ())
    own, received = [], []
    for first, end in ((0, 5 * capacity // 8), (5 * capacity // 8, capacity)):
        patches, send = run(sources=sources, first=first, steps=end - first, before=before, final=True)
        own.append(patches)
        received.append([swap(send, "vis", v) for v in range(1, slabs)])
    tile = place_patches(place_own_kernel, info, place, [], own, tile, per_slab)
    for group in received:
        for patches in group:
            tile = place_patches(place_received_kernel, info, place, [patches], own, tile, per_slab, slabs > 2)
    return tile


def solution(mesh):
    placed = (
        P("chan", "grid", None),
        P(),
        P(("chan", "vis"), None),
        P(("chan", "vis"), None, "grid"),
        P(("chan", "vis"), None, "grid"),
        P("chan", "vis", None, "grid"),
        P(("chan", "vis"), None, "grid"),
    )
    return jax.shard_map(
        shards, mesh=mesh, in_specs=placed, out_specs=P("chan", "grid", "vis"), check_vma=False
    )
```

time: 73.5 us -> 50.3 us (0.68)
  the two profiles are of different devices: /device:TPU:24 before, /device:TPU:16 now
where the time goes in v2:
time: 50.3 us; the launch traced here: 49.9 us
  Pallas kernels  35.3 us (70%)
  waiting for transfers between devices  10.2 us (20%)
  starting transfers between devices  4.28 us (9%)
    pallas_call x3, Pallas kernels, residual(): pl.pallas_call(functools.partial(residual_kernel, sources=number, capacit...  29.1 us
    ppermute x9, waiting for transfers between devices, swap(): return lax.ppermute(array, axis, [(i, i ^ distance) for i in range(size)])  10.2 us
    ppermute x9, starting transfers between devices, swap(): return lax.ppermute(array, axis, [(i, i ^ distance) for i in range(size)])  4.28 us
    pallas_call x3, Pallas kernels, place_patches(): pl.pallas_call(functools.partial(kernel, groups=groups, capacity=capacity...  4.04 us
    pallas_call x1, Pallas kernels, pack(): pl.pallas_call(functools.partial(pack_kernel, count=count, tiles=tiles, p...  2.18 us
  transfers between devices with their start and end apart: 9, of which 6 were waited for; matrix products, arithmetic and copies ran while one was open for 0% of the time, Pallas kernels for 41%

profile of v2, /device:TPU:16, one launch (start us, length us, event | category | flops | bytes accessed | tf_op | source)
XLA Modules:
  0.0 49.9 jit_solution(6287898090133791871)
XLA Ops:
  0.0 0.1 pad_add_fusion.place_ref
  0.1 2.2 %pack_by_tile.1 = (s32[8,128]{1,0:T(8,128)S(1)}, bf16[96,768]{1,0:T(8,128)(2,1)S(1)}, bf16[96,768]{1,0:T(8,128)(2,1)S(1)}, bf16[96,768]{1,0:T(8,128)(2,1)S(1)}, bf16[96,768]{1,0:T(8,128)(2,1)S(1)}) custom-call(s32[2]{0:T(128)S(1)} %pad_add_fusion.place_ref, s32[1,32]{1,0:T(1,128)} %cover_hbm.1, s32[1,32,768]{2,1,0:T(8,128)} %cells_hbm.1, ...), custom_call_target="tpu_custom_call" | custom-call | tf_op jit(solution)/shard_map/pack_by_tile/pallas_call | solution.py:103
  2.3 0.1 collective-permute-start
  2.3 1.6 %collective-permute-start.1 = (bf16[96,768]{1,0:T(8,128)(2,1)S(1)}, bf16[96,768]{1,0:T(8,128)(2,1)S(1)}, u32[]{:S(2)}, u32[]{:S(2)}) collective-permute-start(bf16[96,768]{1,0:T(8,128)(2,1)S(1)} %get-tuple-element.23), channel_id=1, source_target_pairs={{0,4},{2,6},{4,0},{6,2},{8,12},{10,14},{12,8},{14,10},{1,5},{3,7},... | collective-permute-start | bytes 442376 | tf_op jit(solution)/shard_map/ppermute | solution.py:431
  4.0 0.3 collective-permute-start.2
  4.3 1.6 %collective-permute-start.3 = (bf16[96,768]{1,0:T(8,128)(2,1)S(1)}, bf16[96,768]{1,0:T(8,128)(2,1)S(1)}, u32[]{:S(2)}, u32[]{:S(2)}) collective-permute-start(bf16[96,768]{1,0:T(8,128)(2,1)S(1)} %get-tuple-element.25), channel_id=1, source_target_pairs={{0,12},{2,14},{4,8},{6,10},{8,4},{10,6},{12,0},{14,2},{1,13},{3,15... | collective-permute-start | bytes 442376 | tf_op jit(solution)/shard_map/ppermute | solution.py:431
  5.9 0.0 collective-permute-done.refs_1_
  5.9 9.0 %degrid_and_grid.3 = (f32[8,2,128,128]{3,2,1,0:T(8,128)S(1)}, f32[2,128,4096]{2,1,0:T(8,128)}) custom-call(s32[8,128]{1,0:T(8,128)S(1)} %get-tuple-element.20.info_ref, bf16[96,768]{1,0:T(8,128)(2,1)S(1)} %get-tuple-element.21.refs_0_, bf16[96,768]{1,0:T(8,128)(2,1)S(1)} %collective-permute-done.refs_1_, bf16[2,128,8192]{2,1,0:T(8,128)(2,1)} %refs_6_.3, ...), custom_call_target="tpu_custom_call" | custom-call | flops 3221225472 | bytes 524288 | tf_op jit(solution)/shard_map/degrid_and_grid/pallas_call | solution.py:325
  14.9 0.0 collective-permute-done.1.refs_0_
  14.9 0.0 collective-permute-done.2.refs_2_
  14.9 4.4 %collective-permute-done.3.refs_4_ = bf16[96,768]{1,0:T(8,128)(2,1)S(1)} collective-permute-done((bf16[96,768]{1,0:T(8,128)(2,1)S(1)}, bf16[96,768]{1,0:T(8,128)(2,1)S(1)}, u32[]{:S(2)}, u32[]{:S(2)}) %collective-permute-start.3) | collective-permute-done | bytes 147488 | tf_op jit(solution)/shard_map/ppermute | solution.py:431
  19.3 0.0 collective-permute-start.4
  19.3 0.5 %collective-permute-start.5 = (bf16[96,768]{1,0:T(8,128)(2,1)S(1)}, bf16[96,768]{1,0:T(8,128)(2,1)S(1)}, u32[]{:S(2)}, u32[]{:S(2)}) collective-permute-start(bf16[96,768]{1,0:T(8,128)(2,1)S(1)} %collective-permute-done.2.refs_2_), channel_id=1, source_target_pairs={{0,2},{2,0},{4,6},{6,4},{8,10},{10,8},{12,14},{14,12},{1,3},{3,1},... | collective-permute-start | bytes 442376 | tf_op jit(solution)/shard_map/ppermute | solution.py:431
  19.8 0.0 collective-permute-start.6
  19.8 0.9 %collective-permute-done.4.refs_1_ = bf16[96,768]{1,0:T(8,128)(2,1)S(1)} collective-permute-done((bf16[96,768]{1,0:T(8,128)(2,1)S(1)}, bf16[96,768]{1,0:T(8,128)(2,1)S(1)}, u32[]{:S(2)}, u32[]{:S(2)}) %collective-permute-start.4) | collective-permute-done | bytes 147488 | tf_op jit(solution)/shard_map/ppermute | solution.py:431
  20.7 0.2 collective-permute-done.5.refs_3_
  20.9 0.3 collective-permute-done.6.refs_5_
  21.2 12.1 %degrid_and_grid.5 = (f32[5,2,128,128]{3,2,1,0:T(8,128)S(1)}, bf16[5,272,128]{2,1,0:T(8,128)(2,1)S(1)}) custom-call(s32[8,128]{1,0:T(8,128)S(1)} %get-tuple-element.20.info_ref, bf16[96,768]{1,0:T(8,128)(2,1)S(1)} %collective-permute-done.1.refs_0_, bf16[96,768]{1,0:T(8,128)(2,1)S(1)} %collective-permute-done.4.refs_1_, ...), custom_call_target="tpu_custom_call" | custom-call | flops 6039797760 | bytes 327680 | tf_op jit(solution)/shard_map/degrid_and_grid/pallas_call | solution.py:325
  33.3 0.1 collective-permute-start.8
  33.3 8.1 %degrid_and_grid.4 = (f32[3,2,128,128]{3,2,1,0:T(8,128)S(1)}, bf16[3,272,128]{2,1,0:T(8,128)(2,1)S(1)}) custom-call(s32[8,128]{1,0:T(8,128)S(1)} %get-tuple-element.20.info_ref, bf16[96,768]{1,0:T(8,128)(2,1)S(1)} %collective-permute-done.1.refs_0_, bf16[96,768]{1,0:T(8,128)(2,1)S(1)} %collective-permute-done.4.refs_1_, ...), custom_call_target="tpu_custom_call" | custom-call | flops 3623878656 | bytes 196608 | tf_op jit(solution)/shard_map/degrid_and_grid/pallas_call | solution.py:325
  41.4 0.1 collective-permute-start.7
  41.5 1.6 %place_own.1.refs_2_ = f32[2,128,4096]{2,1,0:T(8,128)} custom-call(s32[8,128]{1,0:T(8,128)S(1)} %get-tuple-element.20.info_ref, s32[2]{0:T(128)S(1)} %pad_add_fusion.place_ref, f32[5,2,128,128]{3,2,1,0:T(8,128)S(1)} %get-tuple-element.31.refs_0_, f32[3,2,128,128]{3,2,1,0:T(8,128)S(1)} %get-tuple-element.32.refs_1_, ...), custom_call_target="tpu_custom_call", output_to_operand_aliasing={{}: (4, {})} | custom-call | tf_op jit(solution)/shard_map/place_own/pallas_call | solution.py:413
  43.0 0.5 %collective-permute-done.8.received_ref = bf16[5,272,128]{2,1,0:T(8,128)(2,1)S(1)} collective-permute-done((bf16[5,272,128]{2,1,0:T(8,128)(2,1)S(1)}, bf16[5,272,128]{2,1,0:T(8,128)(2,1)S(1)}, u32[]{:S(2)}, u32[]{:S(2)}) %collective-permute-start.8) | collective-permute-done | bytes 348192 | tf_op jit(solution)/shard_map/ppermute | solution.py:431
  43.6 1.7 %place_received.2.refs_2_ = f32[2,128,4096]{2,1,0:T(8,128)} custom-call(s32[8,128]{1,0:T(8,128)S(1)} %get-tuple-element.20.info_ref, s32[2]{0:T(128)S(1)} %pad_add_fusion.place_ref, bf16[5,272,128]{2,1,0:T(8,128)(2,1)S(1)} %collective-permute-done.8.received_ref, f32[5,2,128,128]{3,2,1,0:T(8,128)S(1)} %get-tuple-element.31.refs_0_, ...), custom_call_target="tpu_custom_call", output_to_operand_aliasing={{}: (5, {})} | custom-call | tf_op jit(solution)/shard_map/place_received/pallas_call | solution.py:413
  45.3 3.8 %collective-permute-done.7.received_ref = bf16[3,272,128]{2,1,0:T(8,128)(2,1)S(1)} collective-permute-done((bf16[3,272,128]{2,1,0:T(8,128)(2,1)S(1)}, bf16[3,272,128]{2,1,0:T(8,128)(2,1)S(1)}, u32[]{:S(2)}, u32[]{:S(2)}) %collective-permute-start.7) | collective-permute-done | bytes 208928 | tf_op jit(solution)/shard_map/ppermute | solution.py:431
  49.1 0.8 %place_received.3 = f32[2,128,4096]{2,1,0:T(8,128)} custom-call(s32[8,128]{1,0:T(8,128)S(1)} %get-tuple-element.20.info_ref, s32[2]{0:T(128)S(1)} %pad_add_fusion.place_ref, bf16[3,272,128]{2,1,0:T(8,128)(2,1)S(1)} %collective-permute-done.7.received_ref, f32[5,2,128,128]{3,2,1,0:T(8,128)S(1)} %get-tuple-element.31.refs_0_, ...), custom_call_target="tpu_custom_call", output_to_operand_aliasing={{}: (5, {})} | custom-call | tf_op jit(solution)/shard_map/place_received/pallas_call | solution.py:413
Async XLA Ops:
  2.3 3.6 %collective-permute-start = (bf16[96,768]{1,0:T(8,128)(2,1)S(1)}, bf16[96,768]{1,0:T(8,128)(2,1)S(1)}, u32[]{:S(2)}, u32[]{:S(2)}) collective-permute-start(bf16[96,768]{1,0:T(8,128)(2,1)S(1)} %get-tuple-element.21.refs_0_), channel_id=1, source_target_pairs={{0,2},{2,0},{4,6},{6,4},{8,10},{10,8},{12,14},{14,12},{1,3},{3,1},... | collective-permute-start | bytes 442376 | tf_op jit(solution)/shard_map/ppermute | solution.py:431
  2.3 12.5 %collective-permute-start.1 = (bf16[96,768]{1,0:T(8,128)(2,1)S(1)}, bf16[96,768]{1,0:T(8,128)(2,1)S(1)}, u32[]{:S(2)}, u32[]{:S(2)}) collective-permute-start(bf16[96,768]{1,0:T(8,128)(2,1)S(1)} %get-tuple-element.23), channel_id=1, source_target_pairs={{0,4},{2,6},{4,0},{6,2},{8,12},{10,14},{12,8},{14,10},{1,5},{3,7},... | collective-permute-start | bytes 442376 | tf_op jit(solution)/shard_map/ppermute | solution.py:431
  4.0 10.9 %collective-permute-start.2 = (bf16[96,768]{1,0:T(8,128)(2,1)S(1)}, bf16[96,768]{1,0:T(8,128)(2,1)S(1)}, u32[]{:S(2)}, u32[]{:S(2)}) collective-permute-start(bf16[96,768]{1,0:T(8,128)(2,1)S(1)} %get-tuple-element.24), channel_id=1, source_target_pairs={{0,8},{2,10},{4,12},{6,14},{8,0},{10,2},{12,4},{14,6},{1,9},{3,11}... | collective-permute-start | bytes 442376 | tf_op jit(solution)/shard_map/ppermute | solution.py:431
  4.3 15.0 %collective-permute-start.3 = (bf16[96,768]{1,0:T(8,128)(2,1)S(1)}, bf16[96,768]{1,0:T(8,128)(2,1)S(1)}, u32[]{:S(2)}, u32[]{:S(2)}) collective-permute-start(bf16[96,768]{1,0:T(8,128)(2,1)S(1)} %get-tuple-element.25), channel_id=1, source_target_pairs={{0,12},{2,14},{4,8},{6,10},{8,4},{10,6},{12,0},{14,2},{1,13},{3,15... | collective-permute-start | bytes 442376 | tf_op jit(solution)/shard_map/ppermute | solution.py:431
  19.3 1.4 %collective-permute-start.4 = (bf16[96,768]{1,0:T(8,128)(2,1)S(1)}, bf16[96,768]{1,0:T(8,128)(2,1)S(1)}, u32[]{:S(2)}, u32[]{:S(2)}) collective-permute-start(bf16[96,768]{1,0:T(8,128)(2,1)S(1)} %collective-permute-done.1.refs_0_), channel_id=1, source_target_pairs={{0,2},{2,0},{4,6},{6,4},{8,10},{10,8},{12,14},{14,12},{1,3},{3,1},... | collective-permute-start | bytes 442376 | tf_op jit(solution)/shard_map/ppermute | solution.py:431
  19.3 1.6 %collective-permute-start.5 = (bf16[96,768]{1,0:T(8,128)(2,1)S(1)}, bf16[96,768]{1,0:T(8,128)(2,1)S(1)}, u32[]{:S(2)}, u32[]{:S(2)}) collective-permute-start(bf16[96,768]{1,0:T(8,128)(2,1)S(1)} %collective-permute-done.2.refs_2_), channel_id=1, source_target_pairs={{0,2},{2,0},{4,6},{6,4},{8,10},{10,8},{12,14},{14,12},{1,3},{3,1},... | collective-permute-start | bytes 442376 | tf_op jit(solution)/shard_map/ppermute | solution.py:431
  19.8 1.4 %collective-permute-start.6 = (bf16[96,768]{1,0:T(8,128)(2,1)S(1)}, bf16[96,768]{1,0:T(8,128)(2,1)S(1)}, u32[]{:S(2)}, u32[]{:S(2)}) collective-permute-start(bf16[96,768]{1,0:T(8,128)(2,1)S(1)} %collective-permute-done.3.refs_4_), channel_id=1, source_target_pairs={{0,2},{2,0},{4,6},{6,4},{8,10},{10,8},{12,14},{14,12},{1,3},{3,1},... | collective-permute-start | bytes 442376 | tf_op jit(solution)/shard_map/ppermute | solution.py:431
  33.3 10.3 %collective-permute-start.8 = (bf16[5,272,128]{2,1,0:T(8,128)(2,1)S(1)}, bf16[5,272,128]{2,1,0:T(8,128)(2,1)S(1)}, u32[]{:S(2)}, u32[]{:S(2)}) collective-permute-start(bf16[5,272,128]{2,1,0:T(8,128)(2,1)S(1)} %get-tuple-element.33), channel_id=1, source_target_pairs={{0,1},{1,0},{2,3},{3,2},{4,5},{5,4},{6,7},{7,6},{8,9},{9,8},{10,11... | collective-permute-start | bytes 1044488 | tf_op jit(solution)/shard_map/ppermute | solution.py:431
  41.4 7.7 %collective-permute-start.7 = (bf16[3,272,128]{2,1,0:T(8,128)(2,1)S(1)}, bf16[3,272,128]{2,1,0:T(8,128)(2,1)S(1)}, u32[]{:S(2)}, u32[]{:S(2)}) collective-permute-start(bf16[3,272,128]{2,1,0:T(8,128)(2,1)S(1)} %get-tuple-element.30), channel_id=1, source_target_pairs={{0,1},{1,0},{2,3},{3,2},{4,5},{5,4},{6,7},{7,6},{8,9},{9,8},{10,11... | collective-permute-start | bytes 626696 | tf_op jit(solution)/shard_map/ppermute | solution.py:431

commit v3 on v2

v3 whole, which is shorter than its diff:
```python
import functools

import jax
import jax.numpy as jnp
from jax import lax
from jax.experimental import pallas as pl
from jax.experimental.pallas import tpu as pltpu
from jax.sharding import PartitionSpec as P

PW = 128
LANES = 128
FIELDS = 5
PLANE_SHIFT = 12
BF16 = jnp.bfloat16
F32 = jnp.float32
I32 = jnp.int32
VMEM_LIMIT = 48 * 1024 * 1024
EMPTY = 255


def round_up(value, unit):
    return -(-value // unit) * unit


def whole_block(shape):
    return pl.BlockSpec(shape, lambda *_: (0,) * len(shape))


def iota(shape, dim):
    return lax.broadcasted_iota(I32, shape, dim)


def pack_kernel(
    place_ref, cover_hbm, cells_hbm, planes_hbm, observed_hbm, weights_hbm, info_ref, *refs,
    count, tiles, per_tile, per_slab, capacity, rows,
):
    outs = refs[: tiles // 2]
    cover_ref, cells_ref, planes_ref, observed_ref, weights_ref, sem = refs[tiles // 2 :]
    sources = (cover_hbm, cells_hbm, planes_hbm, observed_hbm, weights_hbm)
    targets = (cover_ref, cells_ref, planes_ref, observed_ref, weights_ref)
    copies = [pltpu.make_async_copy(x, y, sem.at[i]) for i, (x, y) in enumerate(zip(sources, targets))]
    for copy in copies:
        copy.start()
    me = place_ref[:, 0:1]
    slab = place_ref[:, 1:2]
    copies[0].wait()
    cover_row = cover_ref[...]
    across = jnp.broadcast_to(cover_row, (count, count))
    left = iota((count, count), 0)
    right = iota((count, count), 1)
    cover_col = jnp.sum(jnp.where(left == right, across, 0), axis=1, keepdims=True)

    def order_key(patch, entry):
        owner = patch // per_tile
        foreign = jnp.where((patch - owner * per_tile) // per_slab == slab, 1, 0)
        return owner, foreign * count + entry

    owner_i, key_i = order_key(cover_col, iota((count, 1), 0))
    owner_j, key_j = order_key(cover_row, iota((1, count), 1))
    same = owner_i == owner_j
    rank_row = jnp.sum(jnp.where(same & (key_i < key_j), 1, 0), axis=0, keepdims=True)
    rank_col = jnp.sum(jnp.where(same & (key_j < key_i), 1, 0), axis=1, keepdims=True)

    slot = iota((count, LANES), 1)
    own = (owner_i == me) & (rank_col == slot)
    column = cover_col - owner_i * per_tile
    listed = jnp.sum(jnp.where(own, column + 1, 0), axis=0, keepdims=True)
    total = jnp.sum(jnp.where(owner_i == me, 1, 0), axis=0, keepdims=True)
    lane = iota((1, LANES), 1)
    info = jnp.where(lane < capacity, listed - 1, jnp.where(lane == capacity, total, 0))
    info_ref[...] = jnp.broadcast_to(info, info_ref.shape)

    route = (owner_j ^ me) * capacity + rank_row
    spread = (iota((count, FIELDS * count), 1) % count == iota((count, FIELDS * count), 0)).astype(F32)
    wide = jnp.dot(
        jnp.broadcast_to(route.astype(F32), (8, count)).astype(BF16), spread.astype(BF16),
        preferred_element_type=F32,
    )[0:1].astype(I32)
    field_j = iota((1, FIELDS * count), 1) // count
    for copy in copies[1:]:
        copy.wait()
    cells = cells_ref[0]
    row_off = cells // PW
    plane = planes_ref[0]
    coded = (row_off + PW).astype(F32) * 2.0**-PLANE_SHIFT
    for bit in (1, 2, 4, 8, 16):
        coded = jnp.where((plane & bit) != 0, coded * 2.0**bit, coded)
    fields = [coded, cells - row_off * PW, observed_ref[0, 0], observed_ref[1, 0], weights_ref[0]]
    data = jnp.concatenate([field.astype(F32).astype(BF16) for field in fields], axis=0)
    line = iota((rows, FIELDS * count), 0)
    block = rows // FIELDS
    field_i = line // block
    half = (line - field_i * block) // capacity
    slot_i = (line - field_i * block) - half * capacity
    for m in range(0, tiles, 2):
        pick = (field_i == field_j) & (half < 2) & (wide == (m + half) * capacity + slot_i)
        rows_out = jnp.dot(pick.astype(F32).astype(BF16), data, preferred_element_type=F32)
        outs[m // 2][...] = rows_out.astype(BF16)


def in_hbm(array):
    return pltpu.with_memory_space_constraint(array, pltpu.HBM)


def pack(place, cover, cells, planes, observed, weights, tiles, per_tile, per_slab):
    count, slots = cells.shape[1:]
    capacity = 2 * count // tiles
    rows = FIELDS * round_up(2 * capacity, 16)
    arrays = (cover, cells, planes, observed, weights)
    outputs = [((8, LANES), I32)] + [((rows, slots), BF16)] * (tiles // 2)
    return pl.pallas_call(
        functools.partial(
            pack_kernel, count=count, tiles=tiles, per_tile=per_tile, per_slab=per_slab,
            capacity=capacity, rows=rows,
        ),
        in_specs=[pl.BlockSpec(memory_space=pltpu.VMEM)] + [pl.BlockSpec(memory_space=pltpu.HBM)] * len(arrays),
        out_specs=[pl.BlockSpec(memory_space=pltpu.VMEM)] * len(outputs),
        scratch_shapes=[pltpu.VMEM(a.shape, a.dtype) for a in arrays] + [pltpu.SemaphoreType.DMA((len(arrays),))],
        out_shape=[jax.ShapeDtypeStruct(shape, dtype) for shape, dtype in outputs],
        compiler_params=pltpu.CompilerParams(vmem_limit_bytes=VMEM_LIMIT),
        name="pack_by_tile",
    )(place, *[in_hbm(a) for a in arrays])


def fill_tables(kern_ref, wide_ref, table_ref, support):
    wide_ref[...] = jnp.zeros_like(wide_ref)
    wide_ref[0 : kern_ref.shape[0], 0 : kern_ref.shape[1]] = kern_ref[...]
    flipped = wide_ref[...].T
    zero = jnp.zeros((8 - support, LANES), F32)
    for group in range(4):
        taps = [flipped[support * group + i : support * group + i + 1] for i in reversed(range(support))]
        table_ref[group] = jnp.concatenate([zero, *taps], axis=0)


def pick(array, index, axis):
    return lax.gather(
        array,
        index[..., None],
        lax.GatherDimensionNumbers(
            offset_dims=(), collapsed_slice_dims=(axis,), start_index_map=(axis,),
            operand_batching_dims=(1 - axis,), start_indices_batching_dims=(1 - axis,),
        ),
        slice_sizes=(1, 1),
        mode=lax.GatherScatterMode.PROMISE_IN_BOUNDS,
    )


def tap_places(offset):
    place = jnp.broadcast_to(offset, (16, LANES)) + (15 - iota((16, LANES), 0))
    return place & 7, place >> 3


def wrapped(taps, places):
    return jnp.concatenate([pick(taps, places[0:8], 0), pick(taps, places[8:16], 0)], axis=0)


def expand(ref, base, cols, rows, group):
    for q in range(PW // 16):
        ref[base + 16 * q : base + 16 * q + 16, cols] = jnp.where(group == BF16(2 * q + 1), rows, BF16(0))


def unpack(block_ref, half, capacity, f_ref, i_ref, base):
    block = block_ref.shape[0] // FIELDS
    coded = block_ref[0:block].astype(F32)[half * capacity : (half + 1) * capacity] * 2.0**PLANE_SHIFT
    plane = jnp.zeros_like(coded)
    for bit in (16, 8, 4, 2, 1):
        hit = coded >= PW * 2.0**bit
        coded = jnp.where(hit, coded * 2.0**-bit, coded)
        plane = jnp.where(hit, plane + bit, plane)
    decoded = jnp.concatenate([coded - PW, plane], axis=0)
    decoded = jnp.concatenate([decoded] + [jnp.zeros_like(coded)] * (block // capacity * 2 - 2), axis=0)
    data = jnp.concatenate([decoded.astype(BF16), block_ref[block:]], axis=0)
    shape = (8 * capacity, data.shape[0])
    line = iota(shape, 0)
    field = line & 7
    slot = line >> 3
    start = jnp.where(field == 0, 0, jnp.where(field == 2, capacity, -1))
    first = decoded.shape[0] - block
    later = first + (field - jnp.where(field > 2, 1, 0)) * block + half * capacity
    order = iota(shape, 1) == jnp.where(start >= 0, start, later) + slot
    order = order & (field < FIELDS + 1)
    fields = jnp.dot(order.astype(F32).astype(BF16), data, preferred_element_type=F32)
    whole = fields.astype(I32)
    for slot in range(capacity):
        f_ref[base + slot] = fields[8 * slot : 8 * slot + 8]
        i_ref[base + slot] = whole[8 * slot : 8 * slot + 8]


def degrid_start(i_ref, item, table_ref, wt_ref, u_ref, m_ref, v_ref, g_ref):
    for t in range(u_ref.shape[1] // LANES):
        cols = pl.ds(t * LANES, LANES)
        plane = jnp.broadcast_to(i_ref[item, 2:3, cols], (8, LANES))
        u_place, u_group = tap_places(i_ref[item, 0:1, cols])
        v_place, v_group = tap_places(i_ref[item, 1:2, cols])
        u_re = wrapped(pick(table_ref[0], plane, 1), u_place).astype(BF16)
        u_im = wrapped(pick(table_ref[1], plane, 1), u_place).astype(BF16)
        v_ref[0, :, cols] = wrapped(pick(table_ref[2], plane, 1), v_place)
        v_ref[1, :, cols] = wrapped(pick(table_ref[3], plane, 1), v_place)
        g_ref[:, cols] = v_group
        u_group = u_group.astype(F32).astype(BF16)
        expand(u_ref, 0, cols, u_re, u_group)
        expand(u_ref, PW, cols, u_im, u_group)
    m_ref[...] = jnp.dot(wt_ref[...], u_ref[...], preferred_element_type=F32)


def degrid_end(f_ref, item, u_ref, m_ref, s_ref, v_ref, g_ref, q_ref):
    for t in range(u_ref.shape[1] // LANES):
        cols = pl.ds(t * LANES, LANES)
        group = g_ref[:, cols]
        m_re = jnp.zeros((16, LANES), F32)
        m_im = jnp.zeros((16, LANES), F32)
        for q in range(PW // 16):
            hit = group == 2 * q + 1
            m_re = jnp.where(hit, m_ref[16 * q : 16 * q + 16, cols], m_re)
            m_im = jnp.where(hit, m_ref[PW + 16 * q : PW + 16 * q + 16, cols], m_im)
        v_re = v_ref[0, :, cols]
        v_im = v_ref[1, :, cols]
        model_re = jnp.sum(m_re * v_re - m_im * v_im, axis=0, keepdims=True)
        model_im = jnp.sum(m_re * v_im + m_im * v_re, axis=0, keepdims=True)
        weight = f_ref[item, 5:6, cols]
        res_re = weight * (f_ref[item, 3:4, cols] - model_re)
        res_im = weight * (f_ref[item, 4:5, cols] - model_im)
        s_re = (res_re * v_re + res_im * v_im).astype(BF16)
        s_im = (res_im * v_re - res_re * v_im).astype(BF16)
        group = group.astype(F32).astype(BF16)
        expand(s_ref, 0, cols, s_re, group)
        expand(s_ref, PW, cols, s_im, group)
    q_ref[...] += lax.dot_general(
        u_ref[...], s_ref[...], (((1,), (1,)), ((), ())), preferred_element_type=F32
    )


def residual_kernel(info_ref, *refs, halves, capacity, first, final, begin, zeros, support, unpacked, keep, per):
    refs = list(refs)
    take = lambda number: [refs.pop(0) for _ in range(number)]
    sources = len(halves)
    block_refs = [] if unpacked else take(sources)
    f_ref, i_ref = take(2) if unpacked else (None, None)
    if begin:
        model_refs = take(per)
        (kern_ref,) = take(1)
        patch_ref, tile_ref, wt_ref, table_ref = take(4)
    else:
        wt_ref, table_ref, before_ref = take(3)
        (patch_ref,) = take(1)
    send_ref = take(1)[0] if final else None
    if not unpacked:
        f_ref, i_ref = take(2)
    s_ref, q_ref = take(2)
    u, m, v, g = (take(sources) for _ in range(4))
    step = pl.program_id(0)
    k = first + (step - 1) * per
    if begin:
        wide_ref, zero_ref, sem = take(3)
        total = info_ref[0, capacity]
        width = zero_ref.shape[2]
        clears = [
            pltpu.make_async_copy(zero_ref, tile_ref.at[:, :, pl.ds(i * width, width)], sem.at[i])
            for i in range(zeros)
        ]
    else:
        lane = iota((1, LANES), 1)
        listed = info_ref[0:1]
        total = jnp.sum(jnp.where(lane == capacity, listed, 0))

    def turn():
        for i in range(per if begin else 0):
            slot = jnp.minimum(first + step * per + i, capacity - 1)
            real = model_refs[i][0].T
            imag = model_refs[i][1].T
            wt_ref[slot, 0:PW, 0:PW] = real
            wt_ref[slot, 0:PW, PW:] = -imag
            wt_ref[slot, PW:, 0:PW] = imag
            wt_ref[slot, PW:, PW:] = real

    def start(slot, b):
        degrid_start(i_ref, b * capacity + slot, table_ref, wt_ref.at[slot], u[b], m[b], v[b], g[b])

    def end(slot, b, i):
        degrid_end(f_ref, b * capacity + slot, u[b], m[b], s_ref, v[b], g[b], q_ref.at[i])

    @pl.when(step == 0)
    def _():
        if begin:
            zero_ref[...] = jnp.zeros_like(zero_ref)
            for copy in clears:
                copy.start()
            fill_tables(kern_ref, wide_ref, table_ref, support)
        for b, block_ref in enumerate(block_refs):
            unpack(block_ref, halves[b], capacity, f_ref, i_ref, b * capacity)
        turn()
        start(first, 0)

    @pl.when((step > 0) & (k < total))
    def _():
        turn()
        for i in range(per):
            q_ref[i] = jnp.zeros_like(q_ref[i])
            for b in range(sources):
                end(k + i, b, i)
                if b + 1 < sources:
                    start(k + i, b + 1)
                else:
                    start(jnp.minimum(k + i + 1, capacity - 1), 0)
            out = (step - 1) * per + i
            q_re = q_ref[i, 0:PW, 0:PW] + q_ref[i, PW:, PW:]
            q_im = q_ref[i, 0:PW, PW:] - q_ref[i, PW:, 0:PW]
            if not begin:
                q_re += before_ref[k + i, 0]
                q_im += before_ref[k + i, 1]
            patch_ref[out, 0] = q_re
            patch_ref[out, 1] = q_im
            if final:
                send_ref[out, 0:PW] = q_re.astype(BF16)
                send_ref[out, PW : 2 * PW] = q_im.astype(BF16)

    if final:
        for i in range(per):
            column = jnp.sum(jnp.where(lane == k + i, listed, 0), axis=1, keepdims=True)
            column = jnp.where(k + i < total, column, EMPTY).astype(F32).astype(BF16)
            send_ref[jnp.maximum((step - 1) * per + i, 0), 2 * PW :] = jnp.broadcast_to(column, (16, PW))
    if begin:

        @pl.when(step == pl.num_programs(0) - 1)
        def _():
            for copy in clears:
                copy.wait()


def residual(
    info, sources, capacity, first, steps, model_grid=None, kernels=None, tile_columns=0,
    prepared=None, before=None, final=False, unpacked=None, keep=False, per=1,
):
    begin = prepared is None
    slots = sources[0][0].shape[1]
    number = len(sources)
    in_vmem = pl.BlockSpec(memory_space=pltpu.VMEM)
    operands = [array for array, _ in sources] if unpacked is None else list(unpacked)
    in_specs = [in_vmem for _ in operands]
    out_specs = [in_vmem]
    out_shape = [jax.ShapeDtypeStruct((steps, 2, PW, PW), F32)]
    support, zeros, more = 0, 0, []
    if begin:
        support = kernels.shape[1] // 4
        width = min(tile_columns, 4 * PW)
        zeros = tile_columns // width
        patch_of = lambda s, i, j: (0, 0, jnp.maximum(i[0, jnp.minimum(s * per + j, capacity - 1)], 0))
        in_specs += [pl.BlockSpec((2, PW, PW), functools.partial(patch_of, j=j)) for j in range(per)]
        in_specs.append(whole_block(kernels.shape))
        operands += [in_hbm(model_grid)] * per + [in_hbm(kernels)]
        out_specs += [pl.BlockSpec(memory_space=pltpu.HBM), in_vmem, in_vmem]
        out_shape += [
            jax.ShapeDtypeStruct((2, PW, tile_columns), F32),
            jax.ShapeDtypeStruct((capacity, 2 * PW, 2 * PW), BF16),
            jax.ShapeDtypeStruct((4, 8, LANES), F32),
        ]
        more = [
            pltpu.VMEM((LANES, LANES), F32),
            pltpu.VMEM((2, PW, width), F32),
            pltpu.SemaphoreType.DMA((zeros,)),
        ]
    else:
        in_specs = [in_vmem] + in_specs + [in_vmem] * 3
        operands += [*prepared, before]
    if final:
        out_specs.append(in_vmem)
        out_shape.append(jax.ShapeDtypeStruct((steps, 2 * PW + 16, PW), BF16))
    fields = [((number * capacity, 8, slots), dtype) for dtype in (F32, I32)]
    scratch = [pltpu.VMEM((2 * PW, slots), BF16), pltpu.VMEM((per, 2 * PW, 2 * PW), F32)]
    if keep:
        out_specs += [in_vmem] * 2
        out_shape += [jax.ShapeDtypeStruct(*field) for field in fields]
    elif unpacked is None:
        scratch = [pltpu.VMEM(*field) for field in fields] + scratch
    scratch += [pltpu.VMEM((2 * PW, slots), BF16)] * number
    scratch += [pltpu.VMEM((2 * PW, slots), F32)] * number
    scratch += [pltpu.VMEM((2, 16, slots), F32)] * number
    scratch += [pltpu.VMEM((16, slots), I32)] * number
    return pl.pallas_call(
        functools.partial(
            residual_kernel, halves=tuple(half for _, half in sources), capacity=capacity, first=first,
            final=final, begin=begin, zeros=zeros, support=support, unpacked=unpacked is not None, keep=keep,
            per=per,
        ),
        grid_spec=pltpu.PrefetchScalarGridSpec(
            num_scalar_prefetch=1 if begin else 0, grid=(steps // per + 1,), in_specs=in_specs, out_specs=out_specs,
            scratch_shapes=scratch + more,
        ),
        out_shape=out_shape,
        compiler_params=pltpu.CompilerParams(vmem_limit_bytes=VMEM_LIMIT),
        cost_estimate=pl.CostEstimate(
            flops=steps * number * slots * 16 * PW * PW, bytes_accessed=steps * 65536, transcendentals=0
        ),
        name="degrid_and_grid",
    )(info, *operands)


def place_own_kernel(info_ref, place_ref, *refs, groups, capacity, per_slab):
    own_refs = refs[:groups]
    tile_ref, sem = refs[groups + 1 :]
    slab_start = place_ref[1] * per_slab
    total = info_ref[0, capacity]
    slots = [ref.at[k] for ref in own_refs for k in range(ref.shape[0])]

    def each(act):
        for k in range(capacity):
            local = info_ref[0, k] - slab_start

            @pl.when((k < total) & (local >= 0) & (local < per_slab))
            def _():
                cols = pl.ds(pl.multiple_of(local * PW, PW), PW)
                act(pltpu.make_async_copy(slots[k], tile_ref.at[:, :, cols], sem.at[k]))

    each(lambda copy: copy.start())
    each(lambda copy: copy.wait())


def place_received_kernel(info_ref, place_ref, received_ref, *refs, groups, capacity, per_slab, reread):
    own_refs = refs[:groups]
    tile_ref, sum_ref, sem = refs[groups + 1 :]
    slab_start = place_ref[1] * per_slab
    total = info_ref[0, capacity]
    slots = [ref.at[k] for ref in own_refs for k in range(ref.shape[0])]
    number = received_ref.shape[0]
    columns = [jnp.max(received_ref[k, 2 * PW :].astype(F32)).astype(I32) for k in range(number)]

    def each(act):
        for k in range(number):
            local = columns[k] - slab_start

            @pl.when((local >= 0) & (local < per_slab))
            def _():
                cols = pl.ds(pl.multiple_of(local * PW, PW), PW)
                act(k, pltpu.make_async_copy(sum_ref.at[k], tile_ref.at[:, :, cols], sem.at[k]))

    def send(k, copy):
        if reread:
            cols = pl.ds(pl.multiple_of((columns[k] - slab_start) * PW, PW), PW)
            there = pltpu.make_async_copy(tile_ref.at[:, :, cols], sum_ref.at[k], sem.at[k])
            there.start()
            there.wait()
            sum_ref[k, 0] += received_ref[k, 0:PW].astype(F32)
            sum_ref[k, 1] += received_ref[k, PW : 2 * PW].astype(F32)
            copy.start()
            return
        sum_ref[k, 0] = received_ref[k, 0:PW].astype(F32)
        sum_ref[k, 1] = received_ref[k, PW : 2 * PW].astype(F32)
        for j in range(capacity):

            @pl.when((j < total) & (info_ref[0, j] == columns[k]))
            def _():
                sum_ref[k] += slots[j][...]

        copy.start()

    each(send)
    each(lambda k, copy: copy.wait())


def place_patches(kernel, info, place, received, own, tile, per_slab, reread=False):
    groups = len(own)
    capacity = sum(patches.shape[0] for patches in own)
    scratch = [pltpu.SemaphoreType.DMA((capacity,))]
    if received:
        number, _, width = received[0].shape
        scratch = [pltpu.VMEM((number, 2, tile.shape[1], PW), F32), pltpu.SemaphoreType.DMA((number,))]
        kernel = functools.partial(kernel, reread=reread)
    operands = [*received, *own]
    return pl.pallas_call(
        functools.partial(kernel, groups=groups, capacity=capacity, per_slab=per_slab),
        grid_spec=pltpu.PrefetchScalarGridSpec(
            num_scalar_prefetch=2,
            grid=(1,),
            in_specs=[pl.BlockSpec(memory_space=pltpu.VMEM)] * len(operands)
            + [pl.BlockSpec(memory_space=pltpu.HBM)],
            out_specs=pl.BlockSpec(memory_space=pltpu.HBM),
            scratch_shapes=scratch,
        ),
        out_shape=jax.ShapeDtypeStruct(tile.shape, tile.dtype),
        input_output_aliases={2 + len(operands): 0},
        compiler_params=pltpu.CompilerParams(vmem_limit_bytes=VMEM_LIMIT),
        name="place_received" if received else "place_own",
    )(info, place, *operands, tile)


def swap(array, axis, distance):
    size = lax.axis_size(axis)
    return lax.ppermute(array, axis, [(i, i ^ distance) for i in range(size)])


def shards(model_grid, kernels, cover, cells, planes, observed, weights):
    tiles = lax.axis_size("grid")
    slabs = lax.axis_size("vis")
    per_tile = model_grid.shape[2] // PW
    per_slab = per_tile // slabs
    capacity = 2 * cover.shape[1] // tiles
    place = jnp.stack([lax.axis_index("grid"), lax.axis_index("vis")]).astype(I32)
    lane = lax.broadcasted_iota(I32, (1, LANES), 1)
    places = jnp.where(lane == 0, place[0], place[1])
    info, *pairs = pack(places, cover, cells, planes, observed, weights, tiles, per_tile, per_slab)
    arrived = [swap(pairs[i], "grid", 2 * i) for i in reversed(range(1, tiles // 2))]
    arrived = [pairs[0]] + arrived[::-1]
    both = lambda pair: ((pair, 0), (swap(pair, "grid", 1), 1))
    near = both(arrived[1])
    early = both(arrived[0]) + near[:1]
    before, tile, *prepared = residual(
        info, early, capacity, 0, capacity, model_grid=model_grid, kernels=kernels,
        tile_columns=per_slab * PW, per=2,
    )
    run = functools.partial(residual, info, capacity=capacity, prepared=prepared)
    before, *rest = lax.optimization_barrier((before, *arrived[2:]))
    sources = near[1:] + sum((both(pair) for pair in rest), ())
    while len(sources) > 6:
        (before,) = run(sources[:4], first=0, steps=capacity, before=before)
        sources = sources[4:]
    own, received = [], []
    unpacked = None
    for first, end in ((0, 5 * capacity // 8), (5 * capacity // 8, capacity)):
        patches, send, *fields = run(
            sources, first=first, steps=end - first, before=before, final=True, unpacked=unpacked,
            keep=unpacked is None,
        )
        unpacked = unpacked or fields
        own.append(patches)
        received.append([swap(send, "vis", v) for v in range(1, slabs)])
    tile = place_patches(place_own_kernel, info, place, [], own, tile, per_slab)
    for group in received:
        for patches in group:
            tile = place_patches(place_received_kernel, info, place, [patches], own, tile, per_slab, slabs > 2)
    return tile


def solution(mesh):
    placed = (
        P("chan", "grid", None),
        P(),
        P(("chan", "vis"), None),
        P(("chan", "vis"), None, "grid"),
        P(("chan", "vis"), None, "grid"),
        P("chan", "vis", None, "grid"),
        P(("chan", "vis"), None, "grid"),
    )
    return jax.shard_map(
        shards, mesh=mesh, in_specs=placed, out_specs=P("chan", "grid", "vis"), check_vma=False
    )
```

time: 50.3 us -> 45 us (0.89)
  the two profiles are of different devices: /device:TPU:16 before, /device:TPU:0 now
where the time goes in v3:
time: 45 us; the launch traced here: 44.5 us
  starting transfers between devices  22 us (49%)
  Pallas kernels  11.6 us (26%)
  waiting for transfers between devices  10.8 us (24%)
    ppermute x9, starting transfers between devices, swap(): return lax.ppermute(array, axis, [(i, i ^ distance) for i in range(size)])  22 us
    ppermute x9, waiting for transfers between devices, swap(): return lax.ppermute(array, axis, [(i, i ^ distance) for i in range(size)])  10.8 us
    pallas_call x3, Pallas kernels, residual(): pl.pallas_call(functools.partial(residual_kernel, halves=tuple((half for...  6.97 us
    pallas_call x3, Pallas kernels, place_patches(): pl.pallas_call(functools.partial(kernel, groups=groups, capacity=capacity...  3.08 us
    pallas_call x1, Pallas kernels, pack(): pl.pallas_call(functools.partial(pack_kernel, count=count, tiles=tiles, p...  1.58 us
  transfers between devices with their start and end apart: 9, of which 6 were waited for; matrix products, arithmetic and copies ran while one was open for 0% of the time, Pallas kernels for 17%

profile of v3, /device:TPU:0, one launch (start us, length us, event | category | flops | bytes accessed | tf_op | source)
XLA Modules:
  0.0 44.5 jit_solution(2038634866623627649)
XLA Ops:
  0.0 1.6 %pack_by_tile.1 = (s32[8,128]{1,0:T(8,128)S(1)}, bf16[80,768]{1,0:T(8,128)(2,1)S(1)}, bf16[80,768]{1,0:T(8,128)(2,1)S(1)}, bf16[80,768]{1,0:T(8,128)(2,1)S(1)}, bf16[80,768]{1,0:T(8,128)(2,1)S(1)}) custom-call(s32[1,128]{1,0:T(1,128)S(1)} %compare_select_fusion.place_ref, s32[1,32]{1,0:T(1,128)} %cover_hbm.1, s32[1,32,768]{2,1,0:T(8,128)} %cells_hbm.1, ...), custom_call_target="tpu_custom_call" | custom-call | tf_op jit(solution)/shard_map/pack_by_tile/pallas_call | solution.py:111
  1.6 3.1 %collective-permute-start = (bf16[80,768]{1,0:T(8,128)(2,1)S(1)}, bf16[80,768]{1,0:T(8,128)(2,1)S(1)}, u32[]{:S(2)}, u32[]{:S(2)}) collective-permute-start(bf16[80,768]{1,0:T(8,128)(2,1)S(1)} %get-tuple-element.24), channel_id=1, source_target_pairs={{0,4},{2,6},{4,0},{6,2},{8,12},{10,14},{12,8},{14,10},{1,5},{3,7},... | collective-permute-start | bytes 368648 | tf_op jit(solution)/shard_map/ppermute | solution.py:488
  4.7 0.0 collective-permute-start.2
  4.7 2.6 %collective-permute-start.3 = (bf16[80,768]{1,0:T(8,128)(2,1)S(1)}, bf16[80,768]{1,0:T(8,128)(2,1)S(1)}, u32[]{:S(2)}, u32[]{:S(2)}) collective-permute-start(bf16[80,768]{1,0:T(8,128)(2,1)S(1)} %get-tuple-element.27), channel_id=1, source_target_pairs={{0,8},{2,10},{4,12},{6,14},{8,0},{10,2},{12,4},{14,6},{1,9},{3,11}... | collective-permute-start | bytes 368648 | tf_op jit(solution)/shard_map/ppermute | solution.py:488
  7.3 0.0 collective-permute-start.4
  7.3 0.7 %collective-permute-done.refs_2_ = bf16[80,768]{1,0:T(8,128)(2,1)S(1)} collective-permute-done((bf16[80,768]{1,0:T(8,128)(2,1)S(1)}, bf16[80,768]{1,0:T(8,128)(2,1)S(1)}, u32[]{:S(2)}, u32[]{:S(2)}) %collective-permute-start) | collective-permute-done | bytes 122912 | tf_op jit(solution)/shard_map/ppermute | solution.py:488
  8.0 0.0 collective-permute-done.2.refs_1_
  8.0 3.9 %degrid_and_grid.3 = (f32[8,2,128,128]{3,2,1,0:T(8,128)S(1)}, f32[2,128,4096]{2,1,0:T(8,128)}, bf16[8,256,256]{2,1,0:T(8,128)(2,1)S(1)}, f32[4,8,128]{2,1,0:T(8,128)S(1)}) custom-call(s32[8,128]{1,0:T(8,128)S(1)} %get-tuple-element.23.info_ref, bf16[80,768]{1,0:T(8,128)(2,1)S(1)} %get-tuple-element.25.refs_0_, ...), custom_call_target="tpu_custom_call" | custom-call | flops 4831838208 | bytes 524288 | tf_op jit(solution)/shard_map/degrid_and_grid/pallas_call | solution.py:379
  11.9 5.0 %collective-permute-done.3.refs_1_ = bf16[80,768]{1,0:T(8,128)(2,1)S(1)} collective-permute-done((bf16[80,768]{1,0:T(8,128)(2,1)S(1)}, bf16[80,768]{1,0:T(8,128)(2,1)S(1)}, u32[]{:S(2)}, u32[]{:S(2)}) %collective-permute-start.3) | collective-permute-done | bytes 122912 | tf_op jit(solution)/shard_map/ppermute | solution.py:488
  16.9 0.0 collective-permute-done.4.refs_3_
  16.9 0.8 %collective-permute-start.5 = (bf16[80,768]{1,0:T(8,128)(2,1)S(1)}, bf16[80,768]{1,0:T(8,128)(2,1)S(1)}, u32[]{:S(2)}, u32[]{:S(2)}) collective-permute-start(bf16[80,768]{1,0:T(8,128)(2,1)S(1)} %collective-permute-done.3.refs_1_), channel_id=1, source_target_pairs={{0,2},{2,0},{4,6},{6,4},{8,10},{10,8},{12,14},{14,12},{1,3},{3,1},... | collective-permute-start | bytes 368648 | tf_op jit(solution)/shard_map/ppermute | solution.py:488
  17.7 0.1 collective-permute-start.1
  17.8 0.4 collective-permute-start.6
  18.2 0.8 %collective-permute-done.1.refs_0_ = bf16[80,768]{1,0:T(8,128)(2,1)S(1)} collective-permute-done((bf16[80,768]{1,0:T(8,128)(2,1)S(1)}, bf16[80,768]{1,0:T(8,128)(2,1)S(1)}, u32[]{:S(2)}, u32[]{:S(2)}) %collective-permute-start.1) | collective-permute-done | bytes 122912 | tf_op jit(solution)/shard_map/ppermute | solution.py:488
  19.0 0.0 collective-permute-done.5.refs_2_
  19.0 0.2 collective-permute-done.6.refs_4_
  19.2 1.9 %degrid_and_grid.4 = (f32[5,2,128,128]{3,2,1,0:T(8,128)S(1)}, bf16[5,272,128]{2,1,0:T(8,128)(2,1)S(1)}, f32[40,8,768]{2,1,0:T(8,128)S(1)}, s32[40,8,768]{2,1,0:T(8,128)S(1)}) custom-call(s32[8,128]{1,0:T(8,128)S(1)} %get-tuple-element.23.info_ref, bf16[80,768]{1,0:T(8,128)(2,1)S(1)} %collective-permute-done.1.refs_0_, ...), custom_call_target="tpu_custom_call" | custom-call | flops 5033164800 | bytes 327680 | tf_op jit(solution)/shard_map/degrid_and_grid/pallas_call | solution.py:379
  21.1 10.3 %collective-permute-start.8 = (bf16[5,272,128]{2,1,0:T(8,128)(2,1)S(1)}, bf16[5,272,128]{2,1,0:T(8,128)(2,1)S(1)}, u32[]{:S(2)}, u32[]{:S(2)}) collective-permute-start(bf16[5,272,128]{2,1,0:T(8,128)(2,1)S(1)} %get-tuple-element.39), channel_id=1, source_target_pairs={{0,1},{1,0},{2,3},{3,2},{4,5},{5,4},{6,7},{7,6},{8,9},{9,8},{10,11... | collective-permute-start | bytes 1044488 | tf_op jit(solution)/shard_map/ppermute | solution.py:488
  31.4 1.2 %degrid_and_grid.5 = (f32[3,2,128,128]{3,2,1,0:T(8,128)S(1)}, bf16[3,272,128]{2,1,0:T(8,128)(2,1)S(1)}) custom-call(s32[8,128]{1,0:T(8,128)S(1)} %get-tuple-element.23.info_ref, f32[40,8,768]{2,1,0:T(8,128)S(1)} %get-tuple-element.34.refs_0_, s32[40,8,768]{2,1,0:T(8,128)S(1)} %get-tuple-element.35.refs_1_, ...), custom_call_target="tpu_custom_call" | custom-call | flops 3019898880 | bytes 196608 | tf_op jit(solution)/shard_map/degrid_and_grid/pallas_call | solution.py:379
  32.5 4.7 %collective-permute-start.7 = (bf16[3,272,128]{2,1,0:T(8,128)(2,1)S(1)}, bf16[3,272,128]{2,1,0:T(8,128)(2,1)S(1)}, u32[]{:S(2)}, u32[]{:S(2)}) collective-permute-start(bf16[3,272,128]{2,1,0:T(8,128)(2,1)S(1)} %get-tuple-element.36), channel_id=1, source_target_pairs={{0,1},{1,0},{2,3},{3,2},{4,5},{5,4},{6,7},{7,6},{8,9},{9,8},{10,11... | collective-permute-start | bytes 626696 | tf_op jit(solution)/shard_map/ppermute | solution.py:488
  37.2 0.1 pad_add_fusion.place_ref
  37.3 0.7 %place_own.1.refs_2_ = f32[2,128,4096]{2,1,0:T(8,128)} custom-call(s32[8,128]{1,0:T(8,128)S(1)} %get-tuple-element.23.info_ref, s32[2]{0:T(128)S(1)} %pad_add_fusion.place_ref, f32[5,2,128,128]{3,2,1,0:T(8,128)S(1)} %get-tuple-element.37.refs_0_, f32[3,2,128,128]{3,2,1,0:T(8,128)S(1)} %get-tuple-element.38.refs_1_, ...), custom_call_target="tpu_custom_call", output_to_operand_aliasing={{}: (4, {})} | custom-call | tf_op jit(solution)/shard_map/place_own/pallas_call | solution.py:469
  38.1 2.3 %collective-permute-done.8.received_ref = bf16[5,272,128]{2,1,0:T(8,128)(2,1)S(1)} collective-permute-done((bf16[5,272,128]{2,1,0:T(8,128)(2,1)S(1)}, bf16[5,272,128]{2,1,0:T(8,128)(2,1)S(1)}, u32[]{:S(2)}, u32[]{:S(2)}) %collective-permute-start.8) | collective-permute-done | bytes 348192 | tf_op jit(solution)/shard_map/ppermute | solution.py:488
  40.4 1.6 %place_received.2.refs_2_ = f32[2,128,4096]{2,1,0:T(8,128)} custom-call(s32[8,128]{1,0:T(8,128)S(1)} %get-tuple-element.23.info_ref, s32[2]{0:T(128)S(1)} %pad_add_fusion.place_ref, bf16[5,272,128]{2,1,0:T(8,128)(2,1)S(1)} %collective-permute-done.8.received_ref, f32[5,2,128,128]{3,2,1,0:T(8,128)S(1)} %get-tuple-element.37.refs_0_, ...), custom_call_target="tpu_custom_call", output_to_operand_aliasing={{}: (5, {})} | custom-call | tf_op jit(solution)/shard_map/place_received/pallas_call | solution.py:469
  42.0 1.8 %collective-permute-done.7.received_ref = bf16[3,272,128]{2,1,0:T(8,128)(2,1)S(1)} collective-permute-done((bf16[3,272,128]{2,1,0:T(8,128)(2,1)S(1)}, bf16[3,272,128]{2,1,0:T(8,128)(2,1)S(1)}, u32[]{:S(2)}, u32[]{:S(2)}) %collective-permute-start.7) | collective-permute-done | bytes 208928 | tf_op jit(solution)/shard_map/ppermute | solution.py:488
  43.7 0.8 %place_received.3 = f32[2,128,4096]{2,1,0:T(8,128)} custom-call(s32[8,128]{1,0:T(8,128)S(1)} %get-tuple-element.23.info_ref, s32[2]{0:T(128)S(1)} %pad_add_fusion.place_ref, bf16[3,272,128]{2,1,0:T(8,128)(2,1)S(1)} %collective-permute-done.7.received_ref, f32[5,2,128,128]{3,2,1,0:T(8,128)S(1)} %get-tuple-element.37.refs_0_, ...), custom_call_target="tpu_custom_call", output_to_operand_aliasing={{}: (5, {})} | custom-call | tf_op jit(solution)/shard_map/place_received/pallas_call | solution.py:469
  (1 shorter events, 0.0 us)
Async XLA Ops:
  1.6 6.4 %collective-permute-start = (bf16[80,768]{1,0:T(8,128)(2,1)S(1)}, bf16[80,768]{1,0:T(8,128)(2,1)S(1)}, u32[]{:S(2)}, u32[]{:S(2)}) collective-permute-start(bf16[80,768]{1,0:T(8,128)(2,1)S(1)} %get-tuple-element.24), channel_id=1, source_target_pairs={{0,4},{2,6},{4,0},{6,2},{8,12},{10,14},{12,8},{14,10},{1,5},{3,7},... | collective-permute-start | bytes 368648 | tf_op jit(solution)/shard_map/ppermute | solution.py:488
  4.7 3.3 %collective-permute-start.2 = (bf16[80,768]{1,0:T(8,128)(2,1)S(1)}, bf16[80,768]{1,0:T(8,128)(2,1)S(1)}, u32[]{:S(2)}, u32[]{:S(2)}) collective-permute-start(bf16[80,768]{1,0:T(8,128)(2,1)S(1)} %get-tuple-element.25.refs_0_), channel_id=1, source_target_pairs={{0,2},{2,0},{4,6},{6,4},{8,10},{10,8},{12,14},{14,12},{1,3},{3,1},... | collective-permute-start | bytes 368648 | tf_op jit(solution)/shard_map/ppermute | solution.py:488
  4.7 12.2 %collective-permute-start.3 = (bf16[80,768]{1,0:T(8,128)(2,1)S(1)}, bf16[80,768]{1,0:T(8,128)(2,1)S(1)}, u32[]{:S(2)}, u32[]{:S(2)}) collective-permute-start(bf16[80,768]{1,0:T(8,128)(2,1)S(1)} %get-tuple-element.27), channel_id=1, source_target_pairs={{0,8},{2,10},{4,12},{6,14},{8,0},{10,2},{12,4},{14,6},{1,9},{3,11}... | collective-permute-start | bytes 368648 | tf_op jit(solution)/shard_map/ppermute | solution.py:488
  7.3 9.6 %collective-permute-start.4 = (bf16[80,768]{1,0:T(8,128)(2,1)S(1)}, bf16[80,768]{1,0:T(8,128)(2,1)S(1)}, u32[]{:S(2)}, u32[]{:S(2)}) collective-permute-start(bf16[80,768]{1,0:T(8,128)(2,1)S(1)} %get-tuple-element.28), channel_id=1, source_target_pairs={{0,12},{2,14},{4,8},{6,10},{8,4},{10,6},{12,0},{14,2},{1,13},{3,15... | collective-permute-start | bytes 368648 | tf_op jit(solution)/shard_map/ppermute | solution.py:488
  16.9 2.1 %collective-permute-start.5 = (bf16[80,768]{1,0:T(8,128)(2,1)S(1)}, bf16[80,768]{1,0:T(8,128)(2,1)S(1)}, u32[]{:S(2)}, u32[]{:S(2)}) collective-permute-start(bf16[80,768]{1,0:T(8,128)(2,1)S(1)} %collective-permute-done.3.refs_1_), channel_id=1, source_target_pairs={{0,2},{2,0},{4,6},{6,4},{8,10},{10,8},{12,14},{14,12},{1,3},{3,1},... | collective-permute-start | bytes 368648 | tf_op jit(solution)/shard_map/ppermute | solution.py:488
  17.7 1.3 %collective-permute-start.1 = (bf16[80,768]{1,0:T(8,128)(2,1)S(1)}, bf16[80,768]{1,0:T(8,128)(2,1)S(1)}, u32[]{:S(2)}, u32[]{:S(2)}) collective-permute-start(bf16[80,768]{1,0:T(8,128)(2,1)S(1)} %collective-permute-done.refs_2_), channel_id=1, source_target_pairs={{0,2},{2,0},{4,6},{6,4},{8,10},{10,8},{12,14},{14,12},{1,3},{3,1},... | collective-permute-start | bytes 368648 | tf_op jit(solution)/shard_map/ppermute | solution.py:488
  17.8 1.4 %collective-permute-start.6 = (bf16[80,768]{1,0:T(8,128)(2,1)S(1)}, bf16[80,768]{1,0:T(8,128)(2,1)S(1)}, u32[]{:S(2)}, u32[]{:S(2)}) collective-permute-start(bf16[80,768]{1,0:T(8,128)(2,1)S(1)} %collective-permute-done.4.refs_3_), channel_id=1, source_target_pairs={{0,2},{2,0},{4,6},{6,4},{8,10},{10,8},{12,14},{14,12},{1,3},{3,1},... | collective-permute-start | bytes 368648 | tf_op jit(solution)/shard_map/ppermute | solution.py:488
  21.1 19.3 %collective-permute-start.8 = (bf16[5,272,128]{2,1,0:T(8,128)(2,1)S(1)}, bf16[5,272,128]{2,1,0:T(8,128)(2,1)S(1)}, u32[]{:S(2)}, u32[]{:S(2)}) collective-permute-start(bf16[5,272,128]{2,1,0:T(8,128)(2,1)S(1)} %get-tuple-element.39), channel_id=1, source_target_pairs={{0,1},{1,0},{2,3},{3,2},{4,5},{5,4},{6,7},{7,6},{8,9},{9,8},{10,11... | collective-permute-start | bytes 1044488 | tf_op jit(solution)/shard_map/ppermute | solution.py:488
  32.5 11.2 %collective-permute-start.7 = (bf16[3,272,128]{2,1,0:T(8,128)(2,1)S(1)}, bf16[3,272,128]{2,1,0:T(8,128)(2,1)S(1)}, u32[]{:S(2)}, u32[]{:S(2)}) collective-permute-start(bf16[3,272,128]{2,1,0:T(8,128)(2,1)S(1)} %get-tuple-element.36), channel_id=1, source_target_pairs={{0,1},{1,0},{2,3},{3,2},{4,5},{5,4},{6,7},{7,6},{8,9},{9,8},{10,11... | collective-permute-start | bytes 626696 | tf_op jit(solution)/shard_map/ppermute | solution.py:488
